TPU v7x, 256 devices: a whole 4x4x8 slice. The times are simulated.
256 devices in a mesh: inner: 64 (over x, z, core), outer: 4 (over y).
Axes of the slice: x: 4, y: 4, z: 8, core: 2. Of those that a mesh axis runs over, the one named last changes fastest.
Arguments:
- queries: bfloat16 [4096, 768], P(('inner', 'outer')), may hold values from -8 to 8
- label_rows: float32 [131072, 768], P(('inner', 'outer')), may hold values from -3 to 3
- first_moment: float32 [131072, 768], P(('inner', 'outer')), may hold values from -0.015625 to 0.015625
- second_moment: float32 [131072, 768], P(('inner', 'outer')), may hold values from 1e-07 to 1e-05
- positive_ids: int32 [4096, 8], P(('inner', 'outer')), may hold values from 0 to 131071
- positive_counts: int32 [4096], P(('inner', 'outer')), may hold values from 1 to 8, as said below
Outputs:
- new_rows: float32 [131072, 768], P(('inner', 'outer'))
- new_first: float32 [131072, 768], P(('inner', 'outer'))
- new_second: float32 [131072, 768], P(('inner', 'outer'))
- query_grad: float32 [4096, 768], P(('inner', 'outer'))
- log_total: float32 [4096], P(('inner', 'outer'))
Inputs may be any that keep to these rules, and one draw needn't show every extreme that they name: `positive_counts`: every query has 1 to 8 valid slots, and some query has 8.
All inputs are finite; a program needn't handle non-finite values.
Results may differ from a plain program's by a relative error of at most 0.0003.
The roundings to bfloat16 on the way count: a program that leaves them out, or rounds other values in their place, can miss the bound.
Values may be sent and summed in bfloat16 or wider, within the bound.
A program may use at most 128 MiB of HBM per device.

v0:
```python
import jax
import jax.numpy as jnp
from jax import lax
from jax.sharding import PartitionSpec as P


def combined_all(part, axis, combine):
    gathered = jax.tree.map(lambda a: lax.all_gather(a, axis), part)

    def take(source):
        return jax.tree.map(lambda a: lax.dynamic_index_in_dim(a, source, 0, False), gathered)

    return lax.fori_loop(
        1, lax.axis_size(axis), lambda source, state: combine(state, take(source)), take(0)
    )


def combine_totals(first, second):
    top = jnp.maximum(first[0], second[0])
    total = first[1] * jnp.exp(first[0] - top) + second[1] * jnp.exp(second[0] - top)
    return (top, total)


def targets_for(ids, counts, start, width):
    columns = start + jnp.arange(width, dtype=jnp.int32)[None, :]
    share = jnp.zeros((ids.shape[0], width), jnp.float32)
    for slot_index in range(ids.shape[1]):
        matched = (ids[:, slot_index : slot_index + 1] == columns) & (counts[:, None] > slot_index)
        share = share + matched.astype(jnp.float32)
    return share / counts[:, None].astype(jnp.float32)


def contract_rows(left, right):
    return lax.dot_general(
        left, right, (((1,), (1,)), ((), ())), preferred_element_type=jnp.float32
    )


def contract_columns(left, right):
    return lax.dot_general(
        left, right, (((0,), (0,)), ((), ())), preferred_element_type=jnp.float32
    )


def query_terms(score_grad, rows_bf):
    return jnp.dot(score_grad, rows_bf, preferred_element_type=jnp.float32)


def group_stats(scores):
    local_peak = jnp.max(scores, axis=1)
    peak = lax.pmax(local_peak, "inner")
    local_total = jnp.sum(jnp.exp(scores - peak[:, None]), axis=1)
    total = lax.psum(local_total, "inner")
    return (peak, total)


def adam_update(label_rows, first_moment, second_moment, row_grad):
    new_first = 0.9 * first_moment + 0.1 * row_grad
    new_second = 0.999 * second_moment + 0.001 * row_grad * row_grad
    update = new_first / (1.0 - 0.9**10) / (jnp.sqrt(new_second / (1.0 - 0.999**10)) + 1e-08)
    return (label_rows - 0.001 * update, new_first, new_second)


def shards(queries, label_rows, first_moment, second_moment, positive_ids, positive_counts):
    width = label_rows.shape[0]
    q_dev = queries.shape[0]
    rows_bf = label_rows.astype(jnp.bfloat16)
    owner = lax.axis_index("inner") * lax.axis_size("outer") + lax.axis_index("outer")
    every_query, every_ids, every_counts = (
        lax.all_gather(queries, ("inner", "outer"), axis=0, tiled=True),
        lax.all_gather(positive_ids, ("inner", "outer"), axis=0, tiled=True),
        lax.all_gather(positive_counts, ("inner", "outer"), axis=0, tiled=True),
    )
    scores = contract_rows(every_query, rows_bf)
    group_peak, group_total = group_stats(scores)
    peak, total = combined_all((group_peak, group_total), "outer", combine_totals)
    log_total = peak + jnp.log(total)
    target = targets_for(every_ids, every_counts, owner * width, width)
    score_grad = (jnp.exp(scores - log_total[:, None]) - target).astype(jnp.bfloat16)
    row_grad = contract_columns(score_grad, every_query)
    query_grad = lax.psum_scatter(
        query_terms(score_grad, rows_bf), ("inner", "outer"), scatter_dimension=0, tiled=True
    )
    own_total = lax.dynamic_slice_in_dim(log_total, owner * q_dev, q_dev, 0)
    new_rows, new_first, new_second = adam_update(label_rows, first_moment, second_moment, row_grad)
    return (new_rows, new_first, new_second, query_grad, own_total)


def solution(mesh):
    return jax.shard_map(
        shards,
        mesh=mesh,
        in_specs=(
            P(("inner", "outer"), None),
            P(("inner", "outer"), None),
            P(("inner", "outer"), None),
            P(("inner", "outer"), None),
            P(("inner", "outer"), None),
            P(("inner", "outer")),
        ),
        out_specs=(
            P(("inner", "outer"), None),
            P(("inner", "outer"), None),
            P(("inner", "outer"), None),
            P(("inner", "outer"), None),
            P(("inner", "outer")),
        ),
        check_vma=False,
    )
```

profile of v0, /device:TPU:8, one launch (start us, length us, event | category | flops | bytes accessed | tf_op | source)
XLA Modules:
  0.0 1156.2 jit_solution(16062767333026029905)
XLA Ops:
  7.2 0.0 all-gather.5.cloned.1.call-start
  7.2 0.7 all-gather.5.cloned.1.call-update
  7.9 0.0 reduce-scatter.2.cloned.1.call-start
  8.0 0.9 dynamic-update-slice
  8.8 78.9 %all-reduce = s32[4096]{0:T(1024)S(1)} all-reduce(s32[4096]{0:T(1024)S(1)} %dynamic-update-slice), channel_id=1, replica_groups=mesh['inner'=64,'outer'=4] {'inner','outer'}, use_global_device_ids=true, to_apply=%add | all-reduce | flops 4096 | bytes 32768
  87.7 104.2 %all-gather.2 = s32[256,16,8]{1,2,0:T(8,128)S(1)} all-gather(s32[1,16,8]{1,2,0:T(8,128)} %bitcast.41), channel_id=1, replica_groups=mesh['inner'=64,'outer'=4] {'inner','outer'}, dimensions={0}, use_global_device_ids=true | all-gather | bytes 131584 | tf_op jit(solution)/shard_map/all_gather | solution.py:71
  191.9 0.2 copy.12
  192.1 0.6 reshape.43
  192.8 0.1 fusion.6
  192.9 0.0 all-gather.5.cloned.1.call-done
  192.9 8.5 fusion.7
  201.4 248.8 %pmax.7 = f32[4096]{0:T(1024)S(1)} all-reduce(f32[4096]{0:T(1024)S(1)} %get-tuple-element.173), channel_id=1, replica_groups=mesh['inner'=64,'outer'=4] {'inner'}, use_global_device_ids=true, to_apply=%region_1.0 | all-reduce | flops 4096 | bytes 32768 | tf_op jit(solution)/shard_map/pmax | solution.py:51
  450.2 4.5 exponential_reduce_fusion
  454.7 246.1 %psum.7 = f32[1,4096]{1,0:T(1,128)S(1)} all-reduce(f32[1,4096]{1,0:T(1,128)S(1)} %bitcast.39), channel_id=1, replica_groups=mesh['inner'=64,'outer'=4] {'inner'}, use_global_device_ids=true, to_apply=%region_3.0 | all-reduce | flops 4096 | bytes 32768 | tf_op jit(solution)/shard_map/psum | solution.py:53
  700.9 11.9 %all-gather.1 = f32[4,1,4096]{2,1,0:T(1,128)S(1)} all-gather(f32[1,1,4096]{2,1,0:T(1,128)S(1)} %bitcast.40), channel_id=1, replica_groups=mesh['inner'=64,'outer'=4] {'outer'}, dimensions={0}, use_global_device_ids=true | all-gather | bytes 81920 | tf_op jit(solution)/shard_map/all_gather | solution.py:8
  712.8 12.0 %all-gather = f32[16384]{0:T(1024)S(1)} all-gather(f32[4096]{0:T(1024)S(1)} %pmax.7), channel_id=2, replica_groups=mesh['inner'=64,'outer'=4] {'outer'}, dimensions={0}, use_global_device_ids=true | all-gather | bytes 81920 | tf_op jit(solution)/shard_map/all_gather | solution.py:8
  724.9 0.3 while.17
  725.2 14.4 %subtract_convert_fusion = bf16[4096,512]{0,1:T(8,128)(2,1)S(1)} fusion(f32[4096,512]{0,1:T(8,128)} %get-tuple-element.174, f32[4096]{0:T(1024)S(1)} %convert_element_type.43, s32[4096]{0:T(1024)S(1)} %bitcast.32, s32[4096]{0:T(1024)S(1)} %bitcast.33, s32[4096]{0:T(1024)S(1)} %bitcast.34, s32[4096]{0:T(1024)S(1)} %bitcast.35, s32[4096]{0:T(1024)S(1)} %bitcast.36, ...), kind=kLoop, calls=%fused_computation.3 | loop fusion | flops 73400320 | bytes 12781568 | tf_op jit(solution)/shard_map/convert_element_type | solution.py:79
  739.6 2.0 copy-done
  741.6 6.4 fusion.1
  748.1 0.6 dynamic_slice.32
  748.7 0.8 copy-done.2
  749.5 10.9 multiply_subtract_fusion
  760.4 389.0 %reduce-scatter.2.cloned.1.call-done = f32[16,768]{1,0:T(8,128)} async-done(((f32[4096,768]{1,0:T(8,128)}), f32[16,768]{1,0:T(8,128)}) %reduce-scatter.2.cloned.1.call-update) | async-done | bytes 49168 | tf_op jit(solution)/shard_map/reduce_scatter | solution.py:81
  (20 shorter events, 0.3 us)
Async XLA Ops:
  7.2 185.7 %all-gather.5.cloned.1.call-start = ((), (), s32[]{:S(2)}) async-start(), calls=%async_computation.1 | async-start | bytes 6316032 | tf_op jit(solution)/shard_map/all_gather | solution.py:70
  7.9 1141.4 %reduce-scatter.2.cloned.1.call-start = ((), (), s32[]{:S(2)}) async-start(), calls=%async_computation.2 | async-start | bytes 12632064 | tf_op jit(solution)/shard_map/reduce_scatter | solution.py:81
  87.7 105.2 %copy-start.1 = (f32[512,768]{1,0:T(8,128)S(1)}, f32[512,768]{1,0:T(8,128)}, u32[]{:S(2)}) copy-start(f32[512,768]{1,0:T(8,128)} %param.9) | copy-start | bytes 4718596
  739.6 2.0 copy-start
  748.1 1.4 copy-start.2
Sparse Core Ops, SparseCore 0:
  11.8 118.7 all-gather.4
  748.2 401.0 reduce-scatter.1
where the time goes:
time: 1160 us
  blocking collectives  702 us (61%)
  waiting for transfers between devices  390 us (34%)
  matrix products  25.8 us (2%)
  other arithmetic  19.1 us (2%)
  between operations  14.1 us (1%)
    reduce_scatter x1, waiting for transfers between devices, shards(): lax.psum_scatter(query_terms(score_grad, rows_bf), ('inner', 'outer'), sc...  389 us
    pmax x1, blocking collectives, group_stats(): peak = lax.pmax(local_peak, 'inner')  249 us
    psum x1, blocking collectives, group_stats(): total = lax.psum(local_total, 'inner')  246 us
    all_gather x1, blocking collectives, shards(): lax.all_gather(positive_ids, ('inner', 'outer'), axis=0, tiled=True)  104 us
    unnamed x1, blocking collectives  78.9 us
    all_gather x2, blocking collectives, combined_all(): gathered = jax.tree.map(lambda a: lax.all_gather(a, axis), part)  23.9 us
  transfers between devices with their start and end apart: 2, of which 1 were waited for; matrix products, arithmetic and copies ran while one was open for 1% of the time, Pallas kernels for 0%

commit v1 on v0

v1 whole, which is shorter than its diff:
```python
import functools

import jax
import jax.numpy as jnp
from jax import lax
from jax.experimental import pallas as pl
from jax.experimental.pallas import tpu as pltpu
from jax.sharding import PartitionSpec as P

X, Z = 4, 8
LANES = 128
MESH = pl.DeviceIdType.MESH
ORDERS = ("xyz", "yzx", "zxy")


class Place:
    def __init__(self, sizes):
        self.sizes = sizes
        inner = lax.axis_index("inner")
        self.core = lax.rem(inner, 2)
        self.at = {
            "x": inner // (2 * sizes["z"]),
            "z": lax.rem(inner // 2, sizes["z"]),
            "y": lax.axis_index("outer"),
        }

    def ring(self, axis, delta):
        n = self.sizes[axis]
        return lax.rem(self.at[axis] + delta % n, n)

    def device(self, axis, delta):
        at = dict(self.at)
        core = self.core
        if axis == "core":
            core = 1 - core
        else:
            at[axis] = self.ring(axis, delta)
        return ((at["x"] * self.sizes["z"] + at["z"]) * 2 + core, at["y"])


def slab(ref, half, fixed):
    whole = slice(None)
    first = whole if half is None else half
    return ref.at[(first, *(fixed.get(axis, whole) for axis in "xyz"))]


def steps_of(order, sizes):
    return [(phase, step) for phase, axis in enumerate(order) for step in range(1, sizes[axis] // 2 + 1)]


class Gather:
    def __init__(self, place, part, held, send, recv):
        self.place, self.held, self.send, self.recv = place, held.at[part], send.at[part], recv.at[part]
        self.order = ORDERS[part][::-1]
        self.sent = []

    def copy(self, phase, step, way, origin, device):
        axis = self.order[phase]
        reach = self.place.sizes[axis] // 2
        fixed = {later: self.place.at[later] for later in self.order[phase + 1 :]}
        fixed[axis] = origin
        block = slab(self.held, way if step == reach else None, fixed)
        return pltpu.make_async_remote_copy(
            src_ref=block, dst_ref=block,
            send_sem=self.send.at[phase, way, step - 1], recv_sem=self.recv.at[phase, way, step - 1],
            device_id=device, device_id_type=MESH,
        )

    def arrive(self, phase, step):
        axis = self.order[phase]
        for way, sign in enumerate((1, -1)):
            self.copy(phase, step, way, self.place.ring(axis, -sign * step), self.place.device(axis, sign)).wait_recv()

    def tick(self, phase, step):
        axis = self.order[phase]
        if step > 1:
            self.arrive(phase, step - 1)
        elif phase > 0:
            self.arrive(phase - 1, self.place.sizes[self.order[phase - 1]] // 2)
        for way, sign in enumerate((1, -1)):
            copy = self.copy(phase, step, way, self.place.ring(axis, -sign * (step - 1)), self.place.device(axis, sign))
            copy.start()
            self.sent.append(copy)

    def finish(self):
        last = len(self.order) - 1
        self.arrive(last, self.place.sizes[self.order[last]] // 2)


class Reduce:
    def __init__(self, place, part, total, landing, send, recv):
        self.place, self.total, self.landing = place, total.at[part], landing
        self.send, self.recv = send.at[part], recv.at[part]
        self.order = ORDERS[part]
        self.sent = []

    def block(self, phase, target, half):
        axis = self.order[phase]
        fixed = {done: self.place.at[done] for done in self.order[:phase]}
        fixed[axis] = target
        return slab(self.total, half, fixed)

    def copy(self, phase, step, way, sign):
        axis = self.order[phase]
        reach = self.place.sizes[axis] // 2
        half = way if step == 1 else None
        landed = self.landing[phase].at[way, step - 1]
        return pltpu.make_async_remote_copy(
            src_ref=self.block(phase, self.place.ring(axis, sign * (reach - step + 1)), half),
            dst_ref=landed.at[0] if step == 1 else landed,
            send_sem=self.send.at[phase, way, step - 1], recv_sem=self.recv.at[phase, way, step - 1],
            device_id=self.place.device(axis, sign), device_id_type=MESH,
        )

    def arrive(self, phase, step):
        axis = self.order[phase]
        reach = self.place.sizes[axis] // 2
        for way, sign in enumerate((1, -1)):
            self.copy(phase, step, way, sign).wait_recv()
            half = way if step == 1 else None
            mine = self.block(phase, self.place.ring(axis, sign * (reach - step)), half)
            landed = self.landing[phase].at[way, step - 1]
            if step == 1:
                landed = landed.at[0]
            mine[...] += landed[...]

    def tick(self, phase, step):
        if step > 1:
            self.arrive(phase, step - 1)
        elif phase > 0:
            self.arrive(phase - 1, self.place.sizes[self.order[phase - 1]] // 2)
        for way, sign in enumerate((1, -1)):
            copy = self.copy(phase, step, way, sign)
            copy.start()
            self.sent.append(copy)

    def finish(self):
        last = len(self.order) - 1
        self.arrive(last, self.place.sizes[self.order[last]] // 2)


def exchange(place, axis, source, slots, send, recv):
    copies = []
    for delta in range(1, place.sizes[axis]):
        copy = pltpu.make_async_remote_copy(
            src_ref=source, dst_ref=slots.at[delta - 1],
            send_sem=send.at[delta - 1], recv_sem=recv.at[delta - 1],
            device_id=place.device(axis, delta), device_id_type=MESH,
        )
        copy.start()
        copies.append(copy)
    return copies


def kernel(
    sizes, q_ref, rows_ref, ids_ref, row_grad_ref, query_grad_ref, log_ref,
    rows_bf, held, scores, grads, total, *rest,
):
    landings, rest = rest[:9], rest[9:]
    (ids_z, ids_y, ids_x, ids_zs, ids_ys, stat, stat_x, stat_y, stat_z, logs, factor, row_part, row_land,
     g_send, g_recv, r_send, r_recv, s_send, s_recv, i_send, i_recv, c_send, c_recv) = rest
    place = Place(sizes)
    nx, ny, nz = sizes["x"], sizes["y"], sizes["z"]
    width = rows_ref.shape[0]
    lanes = nz * 16
    at = place.at
    core = place.core

    barrier = pltpu.get_barrier_semaphore()
    peers = [("core", 1)] + [(axis, delta) for axis in "xyz" for delta in range(1, sizes[axis])]
    for axis, delta in peers:
        pl.semaphore_signal(barrier, inc=1, device_id=place.device(axis, delta), device_id_type=MESH)

    own = q_ref[...]
    for piece in range(6):
        held[piece // 2, piece % 2, at["x"], at["y"], at["z"]] = own[:, piece * LANES : (piece + 1) * LANES]
    lane = lax.broadcasted_iota(jnp.int32, (8, lanes), 1)
    own_ids = jnp.where(lane // 16 == at["z"], ids_ref[...], -1)
    ids_zs[...] = own_ids
    rows_bf[core] = rows_ref[...].astype(jnp.bfloat16)

    pl.semaphore_wait(barrier, len(peers))

    gathers = [Gather(place, part, held, g_send, g_recv) for part in range(3)]
    ticks = [steps_of(g.order, sizes) for g in gathers]
    sent = []
    id_copies = exchange(place, "z", ids_zs, ids_z, i_send.at[0], i_recv.at[0])
    sent += id_copies
    for k in range(len(ticks[0])):
        for g, steps in zip(gathers, ticks):
            g.tick(*steps[k])
        if k == 0:
            rows_copy = pltpu.make_async_remote_copy(
                src_ref=rows_bf.at[core], dst_ref=rows_bf.at[core], send_sem=c_send.at[0], recv_sem=c_recv.at[0],
                device_id=place.device("core", 1), device_id_type=MESH,
            )
            rows_copy.start()
        if k == 1:
            merged = own_ids
            for copy in id_copies:
                copy.wait_recv()
            for slot in range(nz - 1):
                merged = jnp.maximum(merged, ids_z[slot])
            ids_ys[at["y"]] = merged
            id_copies = []
            for delta in range(1, ny):
                copy = pltpu.make_async_remote_copy(
                    src_ref=ids_ys.at[at["y"]], dst_ref=ids_ys.at[at["y"]],
                    send_sem=i_send.at[1, delta - 1], recv_sem=i_recv.at[1, delta - 1],
                    device_id=place.device("y", delta), device_id_type=MESH,
                )
                copy.start()
                id_copies.append(copy)
            sent += id_copies
        if k == 2:
            for delta in range(1, ny):
                pltpu.make_async_remote_copy(
                    src_ref=ids_ys.at[at["y"]], dst_ref=ids_ys.at[place.ring("y", -delta)],
                    send_sem=i_send.at[1, delta - 1], recv_sem=i_recv.at[1, delta - 1],
                    device_id=place.device("y", delta), device_id_type=MESH,
                ).wait_recv()
            ids_x[at["x"]] = ids_ys[...]
            for delta in range(1, nx):
                copy = pltpu.make_async_remote_copy(
                    src_ref=ids_x.at[at["x"]], dst_ref=ids_x.at[at["x"]],
                    send_sem=i_send.at[2, delta - 1], recv_sem=i_recv.at[2, delta - 1],
                    device_id=place.device("x", delta), device_id_type=MESH,
                )
                copy.start()
                sent.append(copy)
    for g in gathers:
        g.finish()
    for delta in range(1, nx):
        pltpu.make_async_remote_copy(
            src_ref=ids_x.at[at["x"]], dst_ref=ids_x.at[place.ring("x", -delta)],
            send_sem=i_send.at[2, delta - 1], recv_sem=i_recv.at[2, delta - 1],
            device_id=place.device("x", delta), device_id_type=MESH,
        ).wait_recv()
    rows_copy.wait_recv()

    def queries_of(x, y, count):
        pieces = [held[p // 2, p % 2, x, pl.ds(y, count)].reshape(count * lanes, LANES) for p in range(6)]
        return jnp.concatenate(pieces, axis=1)

    def score_step(x, carry):
        for y in range(0, ny, 2):
            query = queries_of(x, y, 2)
            tops = []
            for side in range(2):
                block = lax.dot_general(
                    rows_bf[side], query, (((1,), (1,)), ((), ())), preferred_element_type=jnp.float32
                )
                tops.append(jnp.max(block, axis=0, keepdims=True))
                for k in range(2):
                    scores[x, y + k, side] = block[:, k * lanes : (k + 1) * lanes]
            top = jnp.maximum(tops[0], tops[1])
            for k in range(2):
                part = top[:, k * lanes : (k + 1) * lanes]
                amount = jnp.zeros((1, lanes), jnp.float32)
                for side in range(2):
                    power = jnp.exp(scores[x, y + k, side] - part)
                    scores[x, y + k, side] = power
                    amount += jnp.sum(power, axis=0, keepdims=True)
                stat[0, 0, x, pl.ds(y + k, 1)] = part
                stat[0, 1, x, pl.ds(y + k, 1)] = amount
        return carry

    lax.fori_loop(0, nx, score_step, 0)

    for stage, (axis, slots) in enumerate((("x", stat_x), ("y", stat_y), ("z", stat_z))):
        copies = exchange(place, axis, stat.at[stage], slots, s_send.at[stage], s_recv.at[stage])
        sent += copies
        for copy in copies:
            copy.wait_recv()
        count = sizes[axis] - 1
        top = stat[stage, 0]
        for slot in range(count):
            top = jnp.maximum(top, slots[slot, 0])
        amount = stat[stage, 1] * jnp.exp(stat[stage, 0] - top)
        for slot in range(count):
            amount += slots[slot, 1] * jnp.exp(slots[slot, 0] - top)
        if stage < 2:
            stat[stage + 1, 0] = top
            stat[stage + 1, 1] = amount
    log_total = top + jnp.log(amount)
    logs[...] = log_total
    factor[...] = jnp.exp(stat[0, 0] - log_total)
    log_ref[...] = jnp.broadcast_to(logs[at["x"], pl.ds(at["y"], 1)], (8, lanes))

    def grad_step(x, carry):
        for y in range(ny):
            ids = ids_x[x, y]
            share = 1.0 / jnp.sum((ids >= 0).astype(jnp.float32), axis=0, keepdims=True)
            scale = factor[x, pl.ds(y, 1)]
            for side in range(2):
                start = (((at["x"] * nz + at["z"]) * 2 + side) * ny + at["y"]) * width
                label = start + lax.broadcasted_iota(jnp.int32, (width, lanes), 0)
                hits = jnp.zeros((width, lanes), jnp.float32)
                for slot in range(8):
                    hits += jnp.where(ids[slot : slot + 1] == label, share, 0.0)
                grads[x, y, side] = (scores[x, y, side] * scale - hits).astype(jnp.bfloat16)
        return carry

    lax.fori_loop(0, nx, grad_step, 0)

    def query_step(x, carry):
        for y in range(0, ny, 2):
            out = None
            for side in range(2):
                left = jnp.concatenate([grads[x, y, side], grads[x, y + 1, side]], axis=1)
                term = lax.dot_general(
                    left, rows_bf[side], (((0,), (0,)), ((), ())), preferred_element_type=jnp.float32
                )
                out = term if out is None else out + term
            for piece in range(6):
                total[piece // 2, piece % 2, x, pl.ds(y, 2)] = out[
                    :, piece * LANES : (piece + 1) * LANES
                ].reshape(2, nz, 16, LANES)
        return carry

    lax.fori_loop(0, nx, query_step, 0)

    def row_side(side, out):
        out[...] = jnp.zeros(out.shape, jnp.float32)

        def step(x, carry):
            left = jnp.concatenate([grads[x, y, side] for y in range(ny)], axis=1)
            out[...] += jnp.dot(left, queries_of(x, 0, ny), preferred_element_type=jnp.float32)
            return carry

        lax.fori_loop(0, nx, step, 0)

    reduces = [
        Reduce(place, part, total, landings[3 * part : 3 * part + 3], r_send, r_recv) for part in range(3)
    ]
    ticks = [steps_of(r.order, sizes) for r in reduces]
    for k in range(len(ticks[0])):
        for r, steps in zip(reduces, ticks):
            r.tick(*steps[k])
        if k == 0:
            row_side(1 - core, row_part)
            row_copy = pltpu.make_async_remote_copy(
                src_ref=row_part, dst_ref=row_land, send_sem=c_send.at[1], recv_sem=c_recv.at[1],
                device_id=place.device("core", 1), device_id_type=MESH,
            )
            row_copy.start()
        if k == 1:
            row_side(core, row_grad_ref)
            row_copy.wait_recv()
            row_grad_ref[...] += row_land[...]
    for r in reduces:
        r.finish()
    for piece in range(6):
        query_grad_ref[:, piece * LANES : (piece + 1) * LANES] = total[
            piece // 2, piece % 2, at["x"], at["y"], at["z"]
        ]
    for group in (*gathers, *reduces):
        sent += group.sent
    for copy in (*sent, rows_copy, row_copy):
        copy.wait_send()


def exchange_step(queries, label_rows, lane_ids, sizes):
    nx, ny, nz = (sizes[axis] for axis in "xyz")
    width, depth = label_rows.shape
    lanes = nz * 16
    f32, bf16 = jnp.float32, jnp.bfloat16
    landings = []
    for order in ORDERS:
        for phase, axis in enumerate(order):
            rest = [sizes[a] for a in "xyz" if a in order[phase + 1 :]]
            landings.append(pltpu.VMEM((2, sizes[axis] // 2, 2, *rest, 16, LANES), f32))
    most = max(sizes.values())
    dma = pltpu.SemaphoreType.DMA
    vmem = pl.BlockSpec(memory_space=pltpu.VMEM)
    return pl.pallas_call(
        functools.partial(kernel, sizes),
        out_shape=(
            jax.ShapeDtypeStruct((width, depth), f32),
            jax.ShapeDtypeStruct((16, depth), f32),
            jax.ShapeDtypeStruct((8, lanes), f32),
        ),
        in_specs=[vmem] * 3,
        out_specs=(vmem,) * 3,
        scratch_shapes=[
            pltpu.VMEM((2, width, depth), bf16),
            pltpu.VMEM((3, 2, nx, ny, nz, 16, LANES), bf16),
            pltpu.VMEM((nx, ny, 2, width, lanes), f32),
            pltpu.VMEM((nx, ny, 2, width, lanes), bf16),
            pltpu.VMEM((3, 2, nx, ny, nz, 16, LANES), f32),
            *landings,
            pltpu.VMEM((nz - 1, 8, lanes), jnp.int32),
            pltpu.VMEM((1, 8, lanes), jnp.int32),
            pltpu.VMEM((nx, ny, 8, lanes), jnp.int32),
            pltpu.VMEM((8, lanes), jnp.int32),
            pltpu.VMEM((ny, 8, lanes), jnp.int32),
            pltpu.VMEM((3, 2, nx, ny, lanes), f32),
            pltpu.VMEM((nx - 1, 2, nx, ny, lanes), f32),
            pltpu.VMEM((ny - 1, 2, nx, ny, lanes), f32),
            pltpu.VMEM((nz - 1, 2, nx, ny, lanes), f32),
            pltpu.VMEM((nx, ny, lanes), f32),
            pltpu.VMEM((nx, ny, lanes), f32),
            pltpu.VMEM((width, depth), f32),
            pltpu.VMEM((width, depth), f32),
            dma((3, 3, 2, most // 2)), dma((3, 3, 2, most // 2)),
            dma((3, 3, 2, most // 2)), dma((3, 3, 2, most // 2)),
            dma((3, most)), dma((3, most)),
            dma((3, most)), dma((3, most)),
            dma((2,)), dma((2,)),
        ],
        compiler_params=pltpu.CompilerParams(
            collective_id=0, has_side_effects=True, vmem_limit_bytes=56 << 20
        ),
        name="classifier_step",
    )(queries, label_rows, lane_ids)


def adam_update(label_rows, first_moment, second_moment, row_grad):
    new_first = 0.9 * first_moment + 0.1 * row_grad
    new_second = 0.999 * second_moment + 0.001 * row_grad * row_grad
    update = new_first / (1.0 - 0.9**10) / (jnp.sqrt(new_second / (1.0 - 0.999**10)) + 1e-08)
    return (label_rows - 0.001 * update, new_first, new_second)


def shards(sizes, queries, label_rows, first_moment, second_moment, positive_ids, positive_counts):
    slots = jnp.arange(positive_ids.shape[1], dtype=jnp.int32)
    valid = jnp.where(slots[None, :] < positive_counts[:, None], positive_ids, -1)
    lane_ids = jnp.tile(valid.T, (1, sizes["z"]))
    row_grad, query_grad, logs = exchange_step(queries, label_rows, lane_ids, sizes)
    z = lax.rem(lax.axis_index("inner") // 2, sizes["z"])
    own_total = lax.dynamic_slice_in_dim(logs[0], z * 16, 16, 0)
    new_rows, new_first, new_second = adam_update(label_rows, first_moment, second_moment, row_grad)
    return (new_rows, new_first, new_second, query_grad, own_total)


def solution(mesh):
    sizes = {"x": X, "y": mesh.shape["outer"], "z": Z}
    rows = P(("inner", "outer"), None)
    return jax.shard_map(
        functools.partial(shards, sizes),
        mesh=mesh,
        in_specs=(rows, rows, rows, rows, rows, P(("inner", "outer"))),
        out_specs=(rows, rows, rows, rows, P(("inner", "outer"))),
        check_vma=False,
    )
```

time: 1160 us -> 132 us (0.11)
  blocking collectives: 702 us -> 0 us
  waiting for transfers between devices: 390 us -> 0 us
  Pallas kernels: 0 us -> 123 us
  matrix products: 25.8 us -> 0 us
  between operations: 14.1 us -> 0.68 us
  other arithmetic: 19.1 us -> 5.97 us
    reduce_scatter x1 -> x0, waiting for transfers between devices: 389 us -> none  [shards(): lax.psum_scatter(query_terms(score_grad, rows_bf), ('inner', 'outer'), sc...]
    pmax x1 -> x0, blocking collectives: 249 us -> none  [group_stats(): peak = lax.pmax(local_peak, 'inner')]
    psum x1 -> x0, blocking collectives: 246 us -> none  [group_stats(): total = lax.psum(local_total, 'inner')]
    all_gather x3 -> x0, blocking collectives: 128 us -> none  [the longest x1 104 us: shards(): lax.all_gather(positive_ids, ('inner', 'outer'), axis=0, tiled=True)]
    pallas_call x0 -> x1, Pallas kernels: none -> 123 us  [exchange_step(): pl.pallas_call(functools.partial(kernel, sizes), out_shape=(jax.ShapeDtyp...]
    unnamed x1 -> x0, blocking collectives: 78.9 us -> none
    dot_general x3 -> x0, matrix products: 25.8 us -> none  [the longest x1 10.9 us: contract_columns(): lax.dot_general(left, right, (((0,), (0,)), ((), ())), preferred_element_...]
    convert_element_type x2 -> x0, other arithmetic: 14.4 us -> none  [the longest x1 14.4 us: shards(): (jnp.exp(scores - log_total[:, None]) - target).astype(jnp.bfloat16)]
  transfers between devices with their start and end apart: 2 -> 0, of which waited for: 1 -> 0; matrix products, arithmetic and copies ran while one was open for 1% -> 0% of each run, Pallas kernels for 0% -> 0%
where the time goes in v1:
time: 132 us
  Pallas kernels  123 us (93%)
  other arithmetic  5.97 us (5%)
  local copies, waits for them, and re-layouts  2.57 us (2%)
    pallas_call x1, Pallas kernels, exchange_step(): pl.pallas_call(functools.partial(kernel, sizes), out_shape=(jax.ShapeDtyp...  123 us
    sub x1, other arithmetic, adam_update(): return (label_rows - 0.001 * update, new_first, new_second)  5.16 us

profile of v1, /device:TPU:8, one launch (start us, length us, event | category | flops | bytes accessed | tf_op | source)
XLA Modules:
  0.0 132.1 jit_solution(11673502634393784725)
XLA Ops:
  0.6 0.0 copy-start
  0.7 0.8 select_bitcast_fusion
  1.5 0.7 tile.10.ids_ref
  2.2 122.9 %classifier_step.1 = (f32[512,768]{1,0:T(8,128)}, f32[16,768]{1,0:T(8,128)}, f32[8,128]{1,0:T(8,128)}) custom-call(bf16[16,768]{1,0:T(8,128)(2,1)} %q_ref.1, f32[512,768]{1,0:T(8,128)} %rows_ref.1, s32[8,128]{1,0:T(8,128)} %tile.10.ids_ref), custom_call_target="tpu_custom_call" | custom-call | tf_op jit(solution)/shard_map/classifier_step/pallas_call | solution.py:376
  125.1 0.7 slice.3
  125.8 0.6 dynamic-slice_bitcast_fusion
  126.4 0.0 copy-done
  126.4 0.0 copy-start.1
  126.4 5.2 %multiply_subtract_fusion = (f32[512,768]{1,0:T(8,128)}, f32[512,768]{1,0:T(8,128)}, f32[512,768]{1,0:T(8,128)}) fusion(f32[512,768]{1,0:T(8,128)S(1)} %copy-done, f32[512,768]{1,0:T(8,128)} %get-tuple-element.8, f32[512,768]{1,0:T(8,128)} %param.8, f32[512,768]{1,0:T(8,128)} %param.9), kind=kLoop, calls=%fused_computation.2 | loop fusion | flops 5111808 | bytes 11010048 | tf_op jit(solution)/shard_map/sub | solution.py:422
  131.5 0.0 copy-done.1
  131.5 0.6 copy.12
  (1 shorter events, 0.0 us)
Async XLA Ops:
  0.6 125.7 %copy-start = (f32[512,768]{1,0:T(8,128)S(1)}, f32[512,768]{1,0:T(8,128)}, u32[]{:S(2)}) copy-start(f32[512,768]{1,0:T(8,128)} %rows_ref.1) | copy-start | bytes 4718596
  126.4 5.2 %copy-start.1 = (f32[16,768]{1,0:T(8,128)S(1)}, f32[16,768]{1,0:T(8,128)}, u32[]{:S(2)}) copy-start(f32[16,768]{1,0:T(8,128)} %get-tuple-element.22) | copy-start | bytes 147460

commit v2 on v1

v2 whole, which is shorter than its diff:
```python
import functools
import heapq
import itertools

import jax
import jax.numpy as jnp
from jax import lax
from jax.experimental import pallas as pl
from jax.experimental.pallas import tpu as pltpu
from jax.sharding import PartitionSpec as P

X, Z = 4, 8
LANES = 128
MESH = pl.DeviceIdType.MESH
ORDERS = ("xyz", "yzx", "zxy")
LINK_RATE = 46.0
COPIES = 256


class Place:
    def __init__(self, sizes):
        self.sizes = sizes
        inner = lax.axis_index("inner")
        self.core = lax.rem(inner, 2)
        self.at = {
            "x": inner // (2 * sizes["z"]),
            "z": lax.rem(inner // 2, sizes["z"]),
            "y": lax.axis_index("outer"),
        }

    def ring(self, axis, delta):
        n = self.sizes[axis]
        return lax.rem(self.at[axis] + delta % n, n)

    def device(self, axis, delta):
        at = dict(self.at)
        core = self.core
        if axis == "core":
            core = 1 - core
        else:
            at[axis] = self.ring(axis, delta)
        return ((at["x"] * self.sizes["z"] + at["z"]) * 2 + core, at["y"])


def slab(ref, half, fixed):
    whole = slice(None)
    first = whole if half is None else half
    return ref.at[(first, *(fixed.get(axis, whole) for axis in "xyz"))]


def offsets(n):
    half = n // 2
    return [0, *(sign * d for d in range(1, half) for sign in (1, -1)), half]


class Message:
    def __init__(self, key, link, kib, hops, deps, copy, landed=None, arrive=None):
        self.key, self.link, self.kib, self.hops, self.deps = key, link, kib, hops, set(deps)
        self.copy, self.landed, self.arrive = copy, landed or copy, arrive


class Job:
    def __init__(self, key, cost, deps, work):
        self.key, self.cost, self.deps, self.work = key, cost, set(deps), work


def play(messages, jobs, leading=()):
    now, free, arrivals, done, sent = 0.0, {}, [], set(), []
    waiting, jobs, leading = list(messages), list(jobs), list(leading)

    def start_ready():
        for message in list(waiting):
            if message.deps <= done:
                waiting.remove(message)
                copy = message.copy()
                copy.start()
                sent.append(copy)
                begin = max(now, free.get(message.link, 0.0))
                free[message.link] = begin + message.kib * message.hops / LINK_RATE
                heapq.heappush(arrivals, (free[message.link] + 0.5 + 0.7 * message.hops, len(sent), message))

    def run(job):
        nonlocal now
        job.work()
        now += job.cost
        done.add(job.key)

    start_ready()
    for job in leading:
        run(job)
        start_ready()
    while arrivals or jobs:
        ready = [job for job in jobs if job.deps <= done]
        prompt = [job for job in ready if job.cost == 0]
        gap = arrivals[0][0] - now if arrivals else 1e9
        if prompt or (ready and gap > 0.6 * ready[0].cost):
            job = (prompt or ready)[0]
            jobs.remove(job)
            run(job)
        else:
            when, _, message = heapq.heappop(arrivals)
            now = max(now, when) + 0.05
            message.landed().wait_recv()
            if message.arrive is not None:
                message.arrive()
                now += message.kib / 2000
            done.add(message.key)
        start_ready()
    assert not waiting
    return sent


class Copies:
    def __init__(self, place, send, recv):
        self.place, self.send, self.recv, self.used = place, send, recv, 0

    def slot(self):
        self.used += 1
        return self.used - 1

    def copy(self, slot, source, target, axis, delta):
        return pltpu.make_async_remote_copy(
            src_ref=source, dst_ref=target, send_sem=self.send.at[slot], recv_sem=self.recv.at[slot],
            device_id=self.place.device(axis, delta), device_id_type=MESH,
        )


def gather_messages(copies, part, held):
    place = copies.place
    held = held.at[part]
    first, second, third = ORDERS[part][::-1]
    at, sizes = place.at, place.sizes
    out = []

    def add(key, axis, delta, kib, hops, deps, block_from):
        slot = copies.slot()
        make = lambda back: copies.copy(slot, block_from(back), block_from(back), axis, delta)
        out.append(Message(
            key, (axis, delta > 0), kib, hops, deps,
            functools.partial(make, 0), functools.partial(make, 1),
        ))

    base = 16 * 2 * LANES * 2 / 1024
    for delta in range(1, sizes[first]):
        far = min(delta, sizes[first] - delta)

        def block(back, delta=delta):
            fixed = dict(at)
            fixed[first] = place.ring(first, -delta * back)
            return slab(held, None, fixed)

        add((part, 1, delta), first, delta, base, far, (), block)
    start = [(part, 1, delta) for delta in range(1, sizes[first])]
    base *= sizes[first]
    reach = sizes[second] // 2
    for step in range(1, reach + 1):
        for way, sign in enumerate((1, -1)):

            def block(back, step=step, way=way, sign=sign):
                fixed = {third: at[third], second: place.ring(second, -sign * (step - 1 + back))}
                return slab(held, way if step == reach else None, fixed)

            deps = start if step == 1 else [(part, 2, way, step - 1)]
            add((part, 2, way, step), second, sign, base / (1 + (step == reach)), 1, deps, block)
    far = sizes[third] // 2
    for offset in offsets(sizes[second]):
        for step in range(1, far + 1):
            for way, sign in enumerate((1, -1)):

                def block(back, offset=offset, step=step, way=way, sign=sign):
                    fixed = {
                        second: place.ring(second, offset),
                        third: place.ring(third, -sign * (step - 1 + back)),
                    }
                    return slab(held, way if step == far else None, fixed)

                if step > 1:
                    deps = [(part, 3, offset, way, step - 1)]
                elif offset == 0:
                    deps = start
                elif abs(offset) == reach:
                    deps = [(part, 2, 0, reach), (part, 2, 1, reach)]
                else:
                    deps = [(part, 2, 0 if offset < 0 else 1, abs(offset))]
                add((part, 3, offset, way, step), third, sign, base / (1 + (step == far)), 1, deps, block)
    return out


def reduce_messages(copies, part, total, landings):
    place = copies.place
    total = total.at[part]
    first, second, third = ORDERS[part]
    at, sizes = place.at, place.sizes
    out = []

    def add(key, axis, delta, kib, hops, deps, source, landed, mine):
        slot = copies.slot()

        def arrive():
            mine()[...] += landed[...]

        out.append(Message(
            key, (axis, delta > 0), kib, hops, deps,
            lambda: copies.copy(slot, source(), landed, axis, delta), None, arrive,
        ))

    base = sizes[third] * 16 * 2 * LANES * 4 / 1024
    reach, far = sizes[first] // 2, sizes[second] // 2
    for number, offset in enumerate(offsets(sizes[second])[::-1]):
        for step in range(1, reach + 1):
            for way, sign in enumerate((1, -1)):

                def block(ahead, offset=offset, step=step, way=way, sign=sign):
                    fixed = {
                        second: place.ring(second, offset),
                        first: place.ring(first, sign * (reach - step + ahead)),
                    }
                    return slab(total, way if step == 1 else None, fixed)

                landed = landings[0].at[number, way, step - 1]
                if step == 1:
                    landed = landed.at[0]
                deps = [(part, 1, offset, way, step - 1)] if step > 1 else []
                ahead = sign * (reach - step + 1)
                planes = [reach if ahead == -reach else ahead] if first == "x" else offsets(sizes["x"])
                deps += [("query", plane) for plane in planes]
                add((part, 1, offset, way, step), first, sign, base / (1 + (step == 1)), 1, deps,
                    functools.partial(block, 1), landed, functools.partial(block, 0))
    for step in range(1, far + 1):
        for way, sign in enumerate((1, -1)):

            def block(ahead, step=step, way=way, sign=sign):
                fixed = {first: at[first], second: place.ring(second, sign * (far - step + ahead))}
                return slab(total, way if step == 1 else None, fixed)

            landed = landings[1].at[way, step - 1]
            if step == 1:
                landed = landed.at[0]
            offset = sign * (far - step + 1)
            if offset == -far:
                offset = far
            deps = [(part, 1, offset, w, reach) for w in range(2)]
            if step > 1:
                deps.append((part, 2, way, step - 1))
            add((part, 2, way, step), second, sign, base / (1 + (step == 1)), 1, deps,
                functools.partial(block, 1), landed, functools.partial(block, 0))
    base /= sizes[third]
    deps = [(part, 1, 0, w, reach) for w in range(2)] + [(part, 2, w, far) for w in range(2)]
    for delta in range(1, sizes[third]):

        def block(ahead, delta=delta):
            fixed = dict(at)
            fixed[third] = place.ring(third, delta * ahead)
            return slab(total, None, fixed)

        add((part, 3, delta), third, delta, base, min(delta, sizes[third] - delta), deps,
            functools.partial(block, 1), landings[2].at[delta - 1], functools.partial(block, 0))
    return out


def exchange(place, axis, source, slots, send, recv):
    copies = []
    for delta in range(1, place.sizes[axis]):
        copy = pltpu.make_async_remote_copy(
            src_ref=source, dst_ref=slots.at[delta - 1],
            send_sem=send.at[delta - 1], recv_sem=recv.at[delta - 1],
            device_id=place.device(axis, delta), device_id_type=MESH,
        )
        copy.start()
        copies.append(copy)
    return copies


def kernel(
    sizes, q_ref, rows_ref, ids_ref, row_grad_ref, query_grad_ref, log_ref,
    rows_bf, held, scores, grads, total, *rest,
):
    landings, rest = rest[:9], rest[9:]
    (ids_z, ids_x, ids_own, ids_ys, stat, stat_x, stat_y, stat_z, logs, factor, row_part, row_land,
     send, recv, s_send, s_recv) = rest
    place = Place(sizes)
    nx, ny, nz = sizes["x"], sizes["y"], sizes["z"]
    width = rows_ref.shape[0]
    lanes = nz * 16
    at = place.at
    core = place.core

    barrier = pltpu.get_barrier_semaphore()
    peers = [("core", 1)] + [(axis, delta) for axis in "xyz" for delta in range(1, sizes[axis])]
    for axis, delta in peers:
        pl.semaphore_signal(barrier, inc=1, device_id=place.device(axis, delta), device_id_type=MESH)

    own = q_ref[...]
    for piece in range(6):
        held[piece // 2, piece % 2, at["x"], at["y"], at["z"]] = own[:, piece * LANES : (piece + 1) * LANES]
    lane = lax.broadcasted_iota(jnp.int32, (8, lanes), 1)
    ids_own[...] = jnp.where(lane // 16 == at["z"], ids_ref[...], -1)
    rows_bf[core] = rows_ref[...].astype(jnp.bfloat16)

    pl.semaphore_wait(barrier, len(peers))

    copies = Copies(place, send, recv)

    def merge_ids():
        merged = ids_own[...]
        for slot in range(nz - 1):
            merged = jnp.maximum(merged, ids_z[slot])
        ids_ys[at["y"]] = merged

    def spread_ids():
        ids_x[at["x"]] = ids_ys[...]

    def count_hits(x):
        def step(y, carry):
            ids = ids_x[x, y]
            for side in range(2):
                start = (((at["x"] * nz + at["z"]) * 2 + side) * ny + at["y"]) * width
                label = start + lax.broadcasted_iota(jnp.int32, (width, lanes), 0)
                hits = jnp.zeros((width, lanes), jnp.float32)
                for slot in range(8):
                    hits += jnp.where(ids[slot : slot + 1] == label, 1.0, 0.0)
                grads[x, y, side] = hits.astype(jnp.bfloat16)
            return carry

        lax.fori_loop(0, ny, step, 0)

    def id_message(kind, axis, delta, kib, source, target, deps):
        slot = copies.slot()
        return Message(
            (kind, delta), (axis, True), kib, min(delta, sizes[axis] - delta), deps,
            lambda: copies.copy(slot, source, target(0), axis, delta),
            lambda: copies.copy(slot, source, target(1), axis, delta),
        )

    messages = [
        id_message("ids1", "z", delta, 4, ids_own, lambda back, delta=delta: ids_z.at[delta - 1], ())
        for delta in range(1, nz)
    ]
    messages += [
        id_message("ids2", "y", delta, 4, ids_ys.at[at["y"]],
                   lambda back, delta=delta: ids_ys.at[place.ring("y", -delta * back)], ["merge"])
        for delta in range(1, ny)
    ]
    messages += [
        id_message("ids3", "x", delta, 16, ids_x.at[at["x"]],
                   lambda back, delta=delta: ids_x.at[place.ring("x", -delta * back)], ["spread"])
        for delta in range(1, nx)
    ]
    parts = [gather_messages(copies, part, held) for part in range(3)]
    messages += [m for group in itertools.zip_longest(*parts) for m in group if m is not None]
    rows_slot = copies.slot()

    def rows_copy():
        return copies.copy(rows_slot, rows_bf.at[core], rows_bf.at[core], "core", 1)

    def rows_landed():
        return copies.copy(rows_slot, rows_bf.at[1 - core], rows_bf.at[1 - core], "core", 1)

    messages.append(Message("rows", ("core", True), width * 1.5 / 4, 1, (), rows_copy, rows_landed))
    jobs = [
        Job("merge", 0, [("ids1", delta) for delta in range(1, nz)], merge_ids),
        Job("spread", 0, ["merge", *(("ids2", delta) for delta in range(1, ny))], spread_ids),
        *(
            Job(("hits", x), 1.5, ["spread", *(("ids3", delta) for delta in range(1, nx))],
                functools.partial(count_hits, x))
            for x in range(nx)
        ),
    ]
    sent = play(messages, jobs)

    def queries_of(x, y, count):
        pieces = [held[p // 2, p % 2, x, pl.ds(y, count)].reshape(count * lanes, LANES) for p in range(6)]
        return jnp.concatenate(pieces, axis=1)

    def score_step(x, carry):
        for y in range(0, ny, 2):
            query = queries_of(x, y, 2)
            tops = []
            for side in range(2):
                block = lax.dot_general(
                    rows_bf[side], query, (((1,), (1,)), ((), ())), preferred_element_type=jnp.float32
                )
                tops.append(jnp.max(block, axis=0, keepdims=True))
                for k in range(2):
                    scores[x, y + k, side] = block[:, k * lanes : (k + 1) * lanes]
            top = jnp.maximum(tops[0], tops[1])
            for k in range(2):
                part = top[:, k * lanes : (k + 1) * lanes]
                amount = jnp.zeros((1, lanes), jnp.float32)
                for side in range(2):
                    power = jnp.exp(scores[x, y + k, side] - part)
                    scores[x, y + k, side] = power
                    amount += jnp.sum(power, axis=0, keepdims=True)
                stat[0, 0, x, pl.ds(y + k, 1)] = part
                stat[0, 1, x, pl.ds(y + k, 1)] = amount
        return carry

    lax.fori_loop(0, nx, score_step, 0)

    for stage, (axis, slots) in enumerate((("x", stat_x), ("y", stat_y), ("z", stat_z))):
        started = exchange(place, axis, stat.at[stage], slots, s_send.at[stage], s_recv.at[stage])
        sent += started
        for copy in started:
            copy.wait_recv()
        count = sizes[axis] - 1
        top = stat[stage, 0]
        for slot in range(count):
            top = jnp.maximum(top, slots[slot, 0])
        amount = stat[stage, 1] * jnp.exp(stat[stage, 0] - top)
        for slot in range(count):
            amount += slots[slot, 1] * jnp.exp(slots[slot, 0] - top)
        if stage < 2:
            stat[stage + 1, 0] = top
            stat[stage + 1, 1] = amount
    log_total = top + jnp.log(amount)
    logs[...] = log_total
    factor[...] = jnp.exp(stat[0, 0] - log_total)
    log_ref[...] = jnp.broadcast_to(logs[at["x"], pl.ds(at["y"], 1)], (8, lanes))

    def query_plane(offset):
        x = place.ring("x", offset)

        def step(pair, carry):
            y = 2 * pair
            out = None
            for side in range(2):
                for k in range(2):
                    share = 1.0 / jnp.sum((ids_x[x, y + k] >= 0).astype(jnp.float32), axis=0, keepdims=True)
                    scale = factor[x, pl.ds(y + k, 1)]
                    hits = grads[x, y + k, side].astype(jnp.float32)
                    grads[x, y + k, side] = (scores[x, y + k, side] * scale - hits * share).astype(jnp.bfloat16)
                left = jnp.concatenate([grads[x, y, side], grads[x, y + 1, side]], axis=1)
                term = lax.dot_general(
                    left, rows_bf[side], (((0,), (0,)), ((), ())), preferred_element_type=jnp.float32
                )
                out = term if out is None else out + term
            for piece in range(6):
                total[piece // 2, piece % 2, x, pl.ds(y, 2)] = out[
                    :, piece * LANES : (piece + 1) * LANES
                ].reshape(2, nz, 16, LANES)
            return carry

        lax.fori_loop(0, ny // 2, step, 0)

    def row_step(side, out, x):
        left = jnp.concatenate([grads[x, y, side] for y in range(ny)], axis=1)
        term = jnp.dot(left, queries_of(x, 0, ny), preferred_element_type=jnp.float32)
        if x == 0:
            out[...] = term
        else:
            out[...] += term

    def row_sum():
        row_grad_ref[...] += row_land[...]

    parts = [
        reduce_messages(copies, part, total, landings[3 * part : 3 * part + 3]) for part in range(3)
    ]
    messages = [m for group in itertools.zip_longest(*parts) for m in group if m is not None]
    row_slot = copies.slot()
    messages.append(Message(
        "row", ("core", True), width * 3 / 4, 1, [("theirs", x) for x in range(nx)],
        lambda: copies.copy(row_slot, row_part, row_land, "core", 1),
    ))
    leading = [
        Job(("query", offset), 2.5, (), functools.partial(query_plane, offset))
        for offset in offsets(nx)[::-1]
    ]
    jobs = [
        Job(("theirs", x), 0.7, (), functools.partial(row_step, 1 - core, row_part, x)) for x in range(nx)
    ] + [
        Job(("ours", x), 0.7, (), functools.partial(row_step, core, row_grad_ref, x)) for x in range(nx)
    ] + [Job("sum", 0.5, ["row", ("ours", nx - 1)], row_sum)]
    sent += play(messages, jobs, leading)
    for piece in range(6):
        query_grad_ref[:, piece * LANES : (piece + 1) * LANES] = total[
            piece // 2, piece % 2, at["x"], at["y"], at["z"]
        ]
    for copy in sent:
        copy.wait_send()


def exchange_step(queries, label_rows, lane_ids, sizes):
    nx, ny, nz = (sizes[axis] for axis in "xyz")
    width, depth = label_rows.shape
    lanes = nz * 16
    f32, bf16 = jnp.float32, jnp.bfloat16
    landings = []
    for first, second, third in ORDERS:
        n1, n2, n3 = sizes[first], sizes[second], sizes[third]
        landings += [
            pltpu.VMEM((n2, 2, n1 // 2, 2, n3, 16, LANES), f32),
            pltpu.VMEM((2, n2 // 2, 2, n3, 16, LANES), f32),
            pltpu.VMEM((n3 - 1, 2, 16, LANES), f32),
        ]
    most = max(sizes.values())
    dma = pltpu.SemaphoreType.DMA
    vmem = pl.BlockSpec(memory_space=pltpu.VMEM)
    return pl.pallas_call(
        functools.partial(kernel, sizes),
        out_shape=(
            jax.ShapeDtypeStruct((width, depth), f32),
            jax.ShapeDtypeStruct((16, depth), f32),
            jax.ShapeDtypeStruct((8, lanes), f32),
        ),
        in_specs=[vmem] * 3,
        out_specs=(vmem,) * 3,
        scratch_shapes=[
            pltpu.VMEM((2, width, depth), bf16),
            pltpu.VMEM((3, 2, nx, ny, nz, 16, LANES), bf16),
            pltpu.VMEM((nx, ny, 2, width, lanes), f32),
            pltpu.VMEM((nx, ny, 2, width, lanes), bf16),
            pltpu.VMEM((3, 2, nx, ny, nz, 16, LANES), f32),
            *landings,
            pltpu.VMEM((nz - 1, 8, lanes), jnp.int32),
            pltpu.VMEM((nx, ny, 8, lanes), jnp.int32),
            pltpu.VMEM((8, lanes), jnp.int32),
            pltpu.VMEM((ny, 8, lanes), jnp.int32),
            pltpu.VMEM((3, 2, nx, ny, lanes), f32),
            pltpu.VMEM((nx - 1, 2, nx, ny, lanes), f32),
            pltpu.VMEM((ny - 1, 2, nx, ny, lanes), f32),
            pltpu.VMEM((nz - 1, 2, nx, ny, lanes), f32),
            pltpu.VMEM((nx, ny, lanes), f32),
            pltpu.VMEM((nx, ny, lanes), f32),
            pltpu.VMEM((width, depth), f32),
            pltpu.VMEM((width, depth), f32),
            dma((COPIES,)), dma((COPIES,)),
            dma((3, most)), dma((3, most)),
        ],
        compiler_params=pltpu.CompilerParams(
            collective_id=0, has_side_effects=True, vmem_limit_bytes=46 << 20
        ),
        name="classifier_step",
    )(queries, label_rows, lane_ids)


def adam_update(label_rows, first_moment, second_moment, row_grad):
    new_first = 0.9 * first_moment + 0.1 * row_grad
    new_second = 0.999 * second_moment + 0.001 * row_grad * row_grad
    update = new_first / (1.0 - 0.9**10) / (jnp.sqrt(new_second / (1.0 - 0.999**10)) + 1e-08)
    return (label_rows - 0.001 * update, new_first, new_second)


def shards(sizes, queries, label_rows, first_moment, second_moment, positive_ids, positive_counts):
    slots = jnp.arange(positive_ids.shape[1], dtype=jnp.int32)
    valid = jnp.where(slots[None, :] < positive_counts[:, None], positive_ids, -1)
    lane_ids = jnp.tile(valid.T, (1, sizes["z"]))
    row_grad, query_grad, logs = exchange_step(queries, label_rows, lane_ids, sizes)
    z = lax.rem(lax.axis_index("inner") // 2, sizes["z"])
    own_total = lax.dynamic_slice_in_dim(logs[0], z * 16, 16, 0)
    new_rows, new_first, new_second = adam_update(label_rows, first_moment, second_moment, row_grad)
    return (new_rows, new_first, new_second, query_grad, own_total)


def solution(mesh):
    sizes = {"x": X, "y": mesh.shape["outer"], "z": Z}
    rows = P(("inner", "outer"), None)
    return jax.shard_map(
        functools.partial(shards, sizes),
        mesh=mesh,
        in_specs=(rows, rows, rows, rows, rows, P(("inner", "outer"))),
        out_specs=(rows, rows, rows, rows, P(("inner", "outer"))),
        check_vma=False,
    )
```

time: 132 us -> 117 us (0.89)
  Pallas kernels: 123 us -> 107 us
    pallas_call x1, Pallas kernels: 123 us -> 107 us  [exchange_step(): pl.pallas_call(functools.partial(kernel, sizes), out_shape=(jax.ShapeDtyp...]
    unnamed x5 -> x7, local copies, waits for them, and re-layouts: 0.63 us -> 2.77 us
where the time goes in v2:
time: 117 us; the launch traced here: 116 us
  Pallas kernels  107 us (91%)
  other arithmetic  4.94 us (4%)
  local copies, waits for them, and re-layouts  3.44 us (3%)
    pallas_call x1, Pallas kernels, exchange_step(): pl.pallas_call(functools.partial(kernel, sizes), out_shape=(jax.ShapeDtyp...  107 us
    sub x1, other arithmetic, adam_update(): return (label_rows - 0.001 * update, new_first, new_second)  4.25 us
    unnamed x7, local copies, waits for them, and re-layouts  2.77 us

profile of v2, /device:TPU:8, one launch (start us, length us, event | category | flops | bytes accessed | tf_op | source)
XLA Modules:
  0.0 116.5 jit_solution(17515336111322943993)
XLA Ops:
  0.7 0.7 select_bitcast_fusion
  1.4 0.1 tile.10.ids_ref
  1.4 0.0 copy-start
  1.4 1.4 %copy-done = f32[512,768]{1,0:T(8,128)S(1)} copy-done((f32[512,768]{1,0:T(8,128)S(1)}, f32[512,768]{1,0:T(8,128)}, u32[]{:S(2)}) %copy-start) | copy-done | bytes 1572888
  2.8 0.0 copy-start.1
  2.8 0.7 copy-done.1
  3.6 0.0 copy-start.2
  3.6 107.4 %classifier_step.1 = (f32[512,768]{1,0:T(8,128)S(1)}, f32[16,768]{1,0:T(8,128)S(1)}, f32[8,128]{1,0:T(8,128)S(1)}) custom-call(bf16[16,768]{1,0:T(8,128)(2,1)S(1)} %copy-done.1, f32[512,768]{1,0:T(8,128)S(1)} %copy-done, s32[8,128]{1,0:T(8,128)S(1)} %tile.10.ids_ref), custom_call_target="tpu_custom_call" | custom-call | tf_op jit(solution)/shard_map/classifier_step/pallas_call | solution.py:499
  111.0 0.6 dynamic-slice_bitcast_fusion
  111.6 0.0 copy-done.2
  111.6 4.2 %multiply_subtract_fusion = (f32[512,768]{1,0:T(8,128)}, f32[512,768]{1,0:T(8,128)}, f32[512,768]{1,0:T(8,128)}) fusion(f32[512,768]{1,0:T(8,128)S(1)} %copy-done, f32[512,768]{1,0:T(8,128)S(1)} %get-tuple-element.8, f32[512,768]{1,0:T(8,128)S(1)} %copy-done.2, f32[512,768]{1,0:T(8,128)} %param.9), kind=kLoop, calls=%fused_computation.2 | loop fusion | flops 5111808 | bytes 11010048 | tf_op jit(solution)/shard_map/sub | solution.py:541
  115.9 0.6 copy.12
  (2 shorter events, 0.0 us)
Async XLA Ops:
  1.4 1.4 %copy-start = (f32[512,768]{1,0:T(8,128)S(1)}, f32[512,768]{1,0:T(8,128)}, u32[]{:S(2)}) copy-start(f32[512,768]{1,0:T(8,128)} %rows_ref.1) | copy-start | bytes 4718596
  2.8 0.7 copy-start.1
  3.6 108.0 %copy-start.2 = (f32[512,768]{1,0:T(8,128)S(1)}, f32[512,768]{1,0:T(8,128)}, u32[]{:S(2)}) copy-start(f32[512,768]{1,0:T(8,128)} %param.8) | copy-start | bytes 4718596

commit v3 on v2

v3 whole, which is shorter than its diff:
```python
import functools
import itertools

import jax
import jax.numpy as jnp
from jax import lax
from jax.experimental import pallas as pl
from jax.experimental.pallas import tpu as pltpu
from jax.sharding import PartitionSpec as P

X, Z = 4, 8
LANES = 128
MESH = pl.DeviceIdType.MESH
ORDERS = ("xyz", "yxz", "zxy")
GATHER_ORDERS = ("zyx", "zxy", "yxz")
LINK_RATE = 46.0
COPIES = 320


class Place:
    def __init__(self, sizes):
        self.sizes = sizes
        inner = lax.axis_index("inner")
        self.core = lax.rem(inner, 2)
        self.at = {
            "x": inner // (2 * sizes["z"]),
            "z": lax.rem(inner // 2, sizes["z"]),
            "y": lax.axis_index("outer"),
        }

    def ring(self, axis, delta):
        n = self.sizes[axis]
        return lax.rem(self.at[axis] + delta % n, n)

    def link(self, axis, delta):
        return (axis, 0 < delta % self.sizes[axis] <= self.sizes[axis] // 2)

    def device(self, axis, delta):
        at = dict(self.at)
        core = self.core
        if axis == "core":
            core = 1 - core
        else:
            at[axis] = self.ring(axis, delta)
        return ((at["x"] * self.sizes["z"] + at["z"]) * 2 + core, at["y"])


def slab(ref, half, fixed):
    whole = slice(None)
    first = whole if half is None else half
    return ref.at[(first, *(fixed.get(axis, whole) for axis in "xyz"))]


def offsets(n):
    half = n // 2
    return [0, *(sign * d for d in range(1, half) for sign in (1, -1)), half]


def offset_of(n, offset):
    return n // 2 if offset == -(n // 2) else offset


class Message:
    def __init__(self, key, link, kib, hops, deps, copy, landed=None, arrive=None, needs=()):
        self.key, self.link, self.kib, self.hops, self.deps = key, link, kib, hops, set(deps)
        self.needs = set(needs)
        self.copy, self.landed, self.arrive = copy, landed or copy, arrive


class Job:
    def __init__(self, key, cost, deps, work, rank=0):
        self.key, self.cost, self.deps, self.work, self.rank = key, cost, set(deps), work, rank


def play(messages, jobs):
    now, free, arrivals, done, sent = 0.0, {}, [], set(), []
    waiting, jobs = list(messages), list(jobs)

    def start_ready():
        for message in list(waiting):
            if message.deps <= done:
                waiting.remove(message)
                copy = message.copy()
                copy.start()
                sent.append(copy)
                begin = max(now, free.get(message.link, 0.0))
                free[message.link] = begin + message.kib * (message.hops if message.hops < 3 else 1.5) / LINK_RATE
                arrivals.append((free[message.link] + 1.4 + 0.6 * message.hops, len(sent), message))

    def run(job):
        nonlocal now
        job.work()
        now += job.cost
        done.add(job.key)

    start_ready()
    while arrivals or jobs:
        landing = sorted(entry for entry in arrivals if entry[2].needs <= done)
        gap = landing[0][0] - now if landing else 1e9
        ready = [job for job in jobs if job.deps <= done and gap > (-1e9, 0.0, 0.6 * job.cost)[job.rank]]
        if ready:
            job = min(ready, key=lambda job: job.rank)
            jobs.remove(job)
            run(job)
        else:
            arrivals.remove(landing[0])
            when, _, message = landing[0]
            now = max(now, when) + 0.05
            message.landed().wait_recv()
            if message.arrive is not None:
                message.arrive()
                now += message.kib / 2000
            done.add(message.key)
        start_ready()
    assert not waiting
    return sent


class Copies:
    def __init__(self, place, send, recv):
        self.place, self.send, self.recv, self.used = place, send, recv, 0

    def slot(self):
        self.used += 1
        return self.used - 1

    def copy(self, slot, source, target, axis, delta):
        return pltpu.make_async_remote_copy(
            src_ref=source, dst_ref=target, send_sem=self.send.at[slot], recv_sem=self.recv.at[slot],
            device_id=self.place.device(axis, delta), device_id_type=MESH,
        )


def reaches(key, offset, n):
    if key == "rows":
        return True
    if key[0] != "in":
        return False
    _, part, phase, *rest = key
    order = GATHER_ORDERS[part]
    if phase < 3:
        return True
    if order[2] == "x":
        _, way, step = rest
        return offset_of(n, step if way else -step) == offset
    return order[1] != "x" or rest[0] == offset


def gather_messages(copies, part, held):
    place = copies.place
    held = held.at[part]
    first, second, third = GATHER_ORDERS[part]
    at, sizes = place.at, place.sizes
    out = []

    def add(key, axis, delta, kib, hops, deps, block_from):
        slot = copies.slot()
        make = lambda back: copies.copy(slot, block_from(back), block_from(back), axis, delta)
        out.append(Message(
            key, place.link(axis, delta), kib, hops, deps,
            functools.partial(make, 0), functools.partial(make, 1),
        ))

    base = 16 * 2 * LANES * 2 / 1024
    for delta in range(1, sizes[first]):
        far = min(delta, sizes[first] - delta)

        def block(back, delta=delta):
            fixed = dict(at)
            fixed[first] = place.ring(first, -delta * back)
            return slab(held, None, fixed)

        add(("in", part, 1, delta), first, delta, base, far, (), block)
    start = [("in", part, 1, delta) for delta in range(1, sizes[first])]
    base *= sizes[first]
    reach = sizes[second] // 2
    for step in range(1, reach + 1):
        for way, sign in enumerate((1, -1)):

            def block(back, step=step, way=way, sign=sign):
                fixed = {third: at[third], second: place.ring(second, -sign * (step - 1 + back))}
                return slab(held, way if step == reach else None, fixed)

            deps = start if step == 1 else [("in", part, 2, way, step - 1)]
            add(("in", part, 2, way, step), second, sign, base / (1 + (step == reach)), 1, deps, block)
    far = sizes[third] // 2
    for offset in offsets(sizes[second]):
        for step in range(1, far + 1):
            for way, sign in enumerate((1, -1)):

                def block(back, offset=offset, step=step, way=way, sign=sign):
                    fixed = {
                        second: place.ring(second, offset),
                        third: place.ring(third, -sign * (step - 1 + back)),
                    }
                    return slab(held, way if step == far else None, fixed)

                if step > 1:
                    deps = [("in", part, 3, offset, way, step - 1)]
                elif offset == 0:
                    deps = start
                elif abs(offset) == reach:
                    deps = [("in", part, 2, 0, reach), ("in", part, 2, 1, reach)]
                else:
                    deps = [("in", part, 2, 0 if offset < 0 else 1, abs(offset))]
                add(("in", part, 3, offset, way, step), third, sign, base / (1 + (step == far)), 1, deps, block)
    return out


def reduce_messages(copies, part, total, landings):
    place = copies.place
    total = total.at[part]
    first, second, third = ORDERS[part]
    at, sizes = place.at, place.sizes
    out = []

    def add(key, axis, delta, kib, hops, deps, source, landed, mine, needs=()):
        slot = copies.slot()

        def arrive():
            mine()[...] += landed[...]

        out.append(Message(
            key, place.link(axis, delta), kib, hops, deps,
            lambda: copies.copy(slot, source(), landed, axis, delta), None, arrive, needs,
        ))

    base = sizes[third] * 16 * 2 * LANES * 4 / 1024
    reach, far = sizes[first] // 2, sizes[second] // 2
    for number, offset in enumerate(offsets(sizes[second])[::-1]):
        for step in range(1, reach + 1):
            for way, sign in enumerate((1, -1)):

                def block(ahead, offset=offset, step=step, way=way, sign=sign):
                    fixed = {
                        second: place.ring(second, offset),
                        first: place.ring(first, sign * (reach - step + ahead)),
                    }
                    return slab(total, way if step == 1 else None, fixed)

                landed = landings[0].at[number, way, step - 1]
                if step == 1:
                    landed = landed.at[0]
                deps = [("out", part, 1, offset, way, step - 1)] if step > 1 else []
                ahead, here = (
                    [offset_of(sizes["x"], sign * (reach - step + k)) for k in (1, 0)] if first == "x" else [offset] * 2
                )
                deps += [("query", ahead)]
                add(("out", part, 1, offset, way, step), first, sign, base / (1 + (step == 1)), 1, deps,
                    functools.partial(block, 1), landed, functools.partial(block, 0), [("query", here)])
    for step in range(1, far + 1):
        for way, sign in enumerate((1, -1)):

            def block(ahead, step=step, way=way, sign=sign):
                fixed = {first: at[first], second: place.ring(second, sign * (far - step + ahead))}
                return slab(total, way if step == 1 else None, fixed)

            landed = landings[1].at[way, step - 1]
            if step == 1:
                landed = landed.at[0]
            offset = offset_of(sizes[second], sign * (far - step + 1))
            deps = [("out", part, 1, offset, w, reach) for w in range(2)]
            if step > 1:
                deps.append(("out", part, 2, way, step - 1))
            add(("out", part, 2, way, step), second, sign, base / (1 + (step == 1)), 1, deps,
                functools.partial(block, 1), landed, functools.partial(block, 0))
    base /= sizes[third]
    deps = [("out", part, 1, 0, w, reach) for w in range(2)] + [("out", part, 2, w, far) for w in range(2)]
    for delta in range(1, sizes[third]):

        def block(ahead, delta=delta):
            fixed = dict(at)
            fixed[third] = place.ring(third, delta * ahead)
            return slab(total, None, fixed)

        add(("out", part, 3, delta), third, delta, base, min(delta, sizes[third] - delta), deps,
            functools.partial(block, 1), landings[2].at[delta - 1], functools.partial(block, 0))
    return out


def kernel(
    sizes, q_ref, rows_ref, ids_ref, count_ref, row_grad_ref, query_grad_ref, log_ref,
    rows_bf, held, scores, grads, total, *rest,
):
    landings, rest = rest[:9], rest[9:]
    (own, rows, ids_in, count_in, ids_z, ids_x, ids_own, ids_ys, stat, stat_x, stat_y, stat_z, logs, factor, row_part, row_land,
     send, recv, load) = rest
    place = Place(sizes)
    nx, ny, nz = sizes["x"], sizes["y"], sizes["z"]
    width = rows_ref.shape[0]
    lanes = nz * 16
    loading = [
        pltpu.make_async_copy(source, target, load.at[k])
        for k, (source, target) in enumerate(
            ((rows_ref, rows), (q_ref, own), (ids_ref, ids_in), (count_ref, count_in))
        )
    ]
    for copy in loading:
        copy.start()
    at = place.at
    core = place.core

    barrier = pltpu.get_barrier_semaphore()
    peers = [("core", 1)] + [(axis, delta) for axis in "xyz" for delta in range(1, sizes[axis])]
    for axis, delta in peers:
        pl.semaphore_signal(barrier, inc=1, device_id=place.device(axis, delta), device_id_type=MESH)

    for copy in loading[1:]:
        copy.wait()
    for piece in range(6):
        held[piece // 2, piece % 2, at["x"], at["y"], at["z"]] = own[:, piece * LANES : (piece + 1) * LANES]
    lane = lax.broadcasted_iota(jnp.int32, (8, lanes), 1)
    valid = lax.broadcasted_iota(jnp.int32, (8, 16), 0) < count_in[...]
    own_ids = jnp.where(valid, ids_in[...], -1)
    ids_own[...] = jnp.where(lane // 16 == at["z"], jnp.concatenate([own_ids] * nz, axis=1), -1)
    loading[0].wait()
    rows_bf[core] = rows[...].astype(jnp.bfloat16)

    pl.semaphore_wait(barrier, len(peers))

    copies = Copies(place, send, recv)

    def merge_ids():
        merged = ids_own[...]
        for slot in range(nz - 1):
            merged = jnp.maximum(merged, ids_z[slot])
        ids_ys[at["y"]] = merged

    def spread_ids():
        ids_x[at["x"]] = ids_ys[...]

    def count_hits(x, y):
        ids = ids_x[x, y]
        start = ((at["x"] * nz + at["z"]) * 2 * ny + at["y"]) * width

        def step(side, carry):
            label = start + side * (ny * width) + lax.broadcasted_iota(jnp.int32, (width, lanes), 0)
            hits = jnp.zeros((width, lanes), jnp.float32)
            for slot in range(8):
                hits += jnp.where(ids[slot : slot + 1] == label, 1.0, 0.0)
            grads[x, y, side] = hits.astype(jnp.bfloat16)
            return carry

        lax.fori_loop(0, 2, step, 0)

    def id_message(kind, axis, delta, kib, source, target, deps):
        slot = copies.slot()
        return Message(
            (kind, delta), place.link(axis, delta), kib, min(delta, sizes[axis] - delta), deps,
            lambda: copies.copy(slot, source, target(0), axis, delta),
            lambda: copies.copy(slot, source, target(1), axis, delta),
        )

    messages = [
        id_message("ids1", "z", delta, 4, ids_own, lambda back, delta=delta: ids_z.at[delta - 1], ())
        for delta in range(1, nz)
    ]
    messages += [
        id_message("ids2", "y", delta, 4, ids_ys.at[at["y"]],
                   lambda back, delta=delta: ids_ys.at[place.ring("y", -delta * back)], ["merge"])
        for delta in range(1, ny)
    ]
    messages += [
        id_message("ids3", "x", delta, 16, ids_x.at[at["x"]],
                   lambda back, delta=delta: ids_x.at[place.ring("x", -delta * back)], ["spread"])
        for delta in range(1, nx)
    ]
    parts = [gather_messages(copies, part, held) for part in range(3)]
    messages += [m for group in itertools.zip_longest(*parts) for m in group if m is not None]
    rows_slot = copies.slot()

    def rows_copy():
        return copies.copy(rows_slot, rows_bf.at[core], rows_bf.at[core], "core", 1)

    def rows_landed():
        return copies.copy(rows_slot, rows_bf.at[1 - core], rows_bf.at[1 - core], "core", 1)

    messages.append(Message("rows", ("core", True), width * 1.5 / 4, 1, (), rows_copy, rows_landed))
    jobs = [
        Job("merge", 0, [("ids1", delta) for delta in range(1, nz)], merge_ids),
        Job("spread", 0, ["merge", *(("ids2", delta) for delta in range(1, ny))], spread_ids),
        *(
            Job(("hits", x, y), 0.4, ["spread", *(("ids3", delta) for delta in range(1, nx))],
                functools.partial(count_hits, x, y), 2)
            for x in range(nx) for y in range(ny)
        ),
    ]
    def queries_of(x, y, count):
        pieces = [held[p // 2, p % 2, x, pl.ds(y, count)].reshape(count * lanes, LANES) for p in range(6)]
        return jnp.concatenate(pieces, axis=1)

    def score_plane(offset):
        x = place.ring("x", offset)
        for y in range(0, ny, 2):
            query = queries_of(x, y, 2)
            tops = []
            for side in range(2):
                block = lax.dot_general(
                    rows_bf[side], query, (((1,), (1,)), ((), ())), preferred_element_type=jnp.float32
                )
                tops.append(jnp.max(block, axis=0, keepdims=True))
                for k in range(2):
                    scores[x, y + k, side] = block[:, k * lanes : (k + 1) * lanes]
            top = jnp.maximum(tops[0], tops[1])
            for k in range(2):
                part = top[:, k * lanes : (k + 1) * lanes]
                amount = jnp.zeros((1, lanes), jnp.float32)
                for side in range(2):
                    power = jnp.exp(scores[x, y + k, side] - part)
                    scores[x, y + k, side] = power
                    amount += jnp.sum(power, axis=0, keepdims=True)
                stat[0, x, 0, y + k : y + k + 1] = part
                stat[0, x, 1, y + k : y + k + 1] = amount

    rings = (("z", stat_z), ("y", stat_y), ("x", stat_x))

    def combine(stage, offset):
        x = slice(None) if offset is None else place.ring("x", offset)
        slots = rings[stage][1]
        count = sizes[rings[stage][0]] - 1
        top = stat[stage, x, 0]
        for slot in range(count):
            top = jnp.maximum(top, slots[slot, x, 0])
        amount = stat[stage, x, 1] * jnp.exp(stat[stage, x, 0] - top)
        for slot in range(count):
            amount += slots[slot, x, 1] * jnp.exp(slots[slot, x, 0] - top)
        if stage < 2:
            stat[stage + 1, x, 0] = top
            stat[stage + 1, x, 1] = amount
        else:
            log_total = top + jnp.log(amount)
            logs[x] = log_total
            factor[x] = jnp.exp(stat[0, x, 0] - log_total)

    def stat_message(stage, offset, delta, deps):
        slot = copies.slot()
        axis, slots = rings[stage]

        def copy():
            x = slice(None) if offset is None else place.ring("x", offset)
            return copies.copy(slot, stat.at[stage, x], slots.at[delta - 1, x], axis, delta)

        return Message(
            ("stat", stage, offset, delta), place.link(axis, delta), 4, min(delta, sizes[axis] - delta), deps, copy
        )

    order = offsets(nx)
    for offset in order:
        deps = [m.key for m in messages if reaches(m.key, offset, sizes["x"])]
        jobs.append(Job(("score", offset), 1.3, deps, functools.partial(score_plane, offset), 1))
    for stage, (axis, _) in enumerate(rings):
        deltas = range(1, sizes[axis])
        for offset in order if stage < 2 else [None]:
            if stage == 0:
                deps = [("score", offset)]
            elif stage == 1:
                deps = [("combine", 0, offset)]
            else:
                deps = [("combine", 1, offset) for offset in order]
            messages += [stat_message(stage, offset, delta, deps) for delta in deltas]
            jobs.append(Job(
                ("combine", stage, offset), 0.2, [("stat", stage, offset, delta) for delta in deltas],
                functools.partial(combine, stage, offset),
            ))

    order = order[::-1]

    def query_plane(offset):
        x = place.ring("x", offset)

        def step(pair, carry):
            y = 2 * pair
            out = None
            for side in range(2):
                for k in range(2):
                    share = 1.0 / jnp.sum((ids_x[x, y + k] >= 0).astype(jnp.float32), axis=0, keepdims=True)
                    scale = factor[x, pl.ds(y + k, 1)]
                    hits = grads[x, y + k, side].astype(jnp.float32)
                    grads[x, y + k, side] = (scores[x, y + k, side] * scale - hits * share).astype(jnp.bfloat16)
                left = jnp.concatenate([grads[x, y, side], grads[x, y + 1, side]], axis=1)
                term = lax.dot_general(
                    left, rows_bf[side], (((0,), (0,)), ((), ())), preferred_element_type=jnp.float32
                )
                out = term if out is None else out + term
            for piece in range(6):
                total[piece // 2, piece % 2, x, pl.ds(y, 2)] = out[
                    :, piece * LANES : (piece + 1) * LANES
                ].reshape(2, nz, 16, LANES)
            return carry

        lax.fori_loop(0, ny // 2, step, 0)

    def row_step(side, out, offset):
        x = place.ring("x", offset)
        left = jnp.concatenate([grads[x, y, side] for y in range(ny)], axis=1)
        term = jnp.dot(left, queries_of(x, 0, ny), preferred_element_type=jnp.float32)
        if offset == order[0]:
            out[...] = term
        else:
            out[...] += term

    def row_sum():
        row_grad_ref[...] += row_land[...]

    parts = [
        reduce_messages(copies, part, total, landings[3 * part : 3 * part + 3]) for part in range(3)
    ]
    messages += [m for group in itertools.zip_longest(*parts) for m in group if m is not None]
    row_slot = copies.slot()
    messages.append(Message(
        "row", ("core", True), width * 3 / 4, 1, [("theirs", order[-1])],
        lambda: copies.copy(row_slot, row_part, row_land, "core", 1),
    ))
    every_hit = [("hits", x, y) for x in range(nx) for y in range(ny)]
    jobs += [
        Job(("query", offset), 3.0, [("combine", 2, None), *every_hit], functools.partial(query_plane, offset), 1)
        for offset in order
    ]
    for name, side, out in (("theirs", 1 - core, row_part), ("ours", core, row_grad_ref)):
        before = []
        for offset in order:
            jobs.append(Job(
                (name, offset), 0.7, [("query", offset), *before], functools.partial(row_step, side, out, offset), 2
            ))
            before = [(name, offset)]
    jobs.append(Job("sum", 0.5, ["row", ("ours", order[-1])], row_sum, 2))
    sent = play(messages, jobs)
    log_ref[...] = jnp.broadcast_to(logs[at["x"], pl.ds(at["y"], 1)], (8, lanes))
    for piece in range(6):
        query_grad_ref[:, piece * LANES : (piece + 1) * LANES] = total[
            piece // 2, piece % 2, at["x"], at["y"], at["z"]
        ]
    for copy in sent:
        copy.wait_send()


def exchange_step(queries, label_rows, slot_ids, counts, sizes):
    nx, ny, nz = (sizes[axis] for axis in "xyz")
    width, depth = label_rows.shape
    lanes = nz * 16
    f32, bf16 = jnp.float32, jnp.bfloat16
    landings = []
    for first, second, third in ORDERS:
        n1, n2, n3 = sizes[first], sizes[second], sizes[third]
        landings += [
            pltpu.VMEM((n2, 2, n1 // 2, 2, n3, 16, LANES), f32),
            pltpu.VMEM((2, n2 // 2, 2, n3, 16, LANES), f32),
            pltpu.VMEM((n3 - 1, 2, 16, LANES), f32),
        ]
    dma = pltpu.SemaphoreType.DMA
    vmem = pl.BlockSpec(memory_space=pltpu.VMEM)
    return pl.pallas_call(
        functools.partial(kernel, sizes),
        out_shape=(
            jax.ShapeDtypeStruct((width, depth), f32),
            jax.ShapeDtypeStruct((16, depth), f32),
            jax.ShapeDtypeStruct((8, lanes), f32),
        ),
        in_specs=[pl.BlockSpec(memory_space=pltpu.HBM)] * 4,
        out_specs=(vmem,) * 3,
        scratch_shapes=[
            pltpu.VMEM((2, width, depth), bf16),
            pltpu.VMEM((3, 2, nx, ny, nz, 16, LANES), bf16),
            pltpu.VMEM((nx, ny, 2, width, lanes), f32),
            pltpu.VMEM((nx, ny, 2, width, lanes), bf16),
            pltpu.VMEM((3, 2, nx, ny, nz, 16, LANES), f32),
            *landings,
            pltpu.VMEM((16, depth), bf16),
            pltpu.VMEM((width, depth), f32),
            pltpu.VMEM((8, 16), jnp.int32),
            pltpu.VMEM((1, 16), jnp.int32),
            pltpu.VMEM((nz - 1, 8, lanes), jnp.int32),
            pltpu.VMEM((nx, ny, 8, lanes), jnp.int32),
            pltpu.VMEM((8, lanes), jnp.int32),
            pltpu.VMEM((ny, 8, lanes), jnp.int32),
            pltpu.VMEM((3, nx, 2, ny, lanes), f32),
            pltpu.VMEM((nx - 1, nx, 2, ny, lanes), f32),
            pltpu.VMEM((ny - 1, nx, 2, ny, lanes), f32),
            pltpu.VMEM((nz - 1, nx, 2, ny, lanes), f32),
            pltpu.VMEM((nx, ny, lanes), f32),
            pltpu.VMEM((nx, ny, lanes), f32),
            pltpu.VMEM((width, depth), f32),
            pltpu.VMEM((width, depth), f32),
            dma((COPIES,)), dma((COPIES,)), dma((4,)),
        ],
        compiler_params=pltpu.CompilerParams(
            collective_id=0, has_side_effects=True, vmem_limit_bytes=46 << 20
        ),
        name="classifier_step",
    )(queries, label_rows, slot_ids, counts)


def adam_update(label_rows, first_moment, second_moment, row_grad):
    new_first = 0.9 * first_moment + 0.1 * row_grad
    new_second = 0.999 * second_moment + 0.001 * row_grad * row_grad
    update = new_first / (1.0 - 0.9**10) / (jnp.sqrt(new_second / (1.0 - 0.999**10)) + 1e-08)
    return (label_rows - 0.001 * update, new_first, new_second)


def shards(sizes, queries, label_rows, first_moment, second_moment, positive_ids, positive_counts):
    row_grad, query_grad, logs = exchange_step(
        queries, label_rows, positive_ids.T, positive_counts.reshape(1, -1), sizes
    )
    z = lax.rem(lax.axis_index("inner") // 2, sizes["z"])
    own_total = lax.dynamic_slice_in_dim(logs[0], z * 16, 16, 0)
    new_rows, new_first, new_second = adam_update(label_rows, first_moment, second_moment, row_grad)
    return (new_rows, new_first, new_second, query_grad, own_total)


def solution(mesh):
    sizes = {"x": X, "y": mesh.shape["outer"], "z": Z}
    rows = P(("inner", "outer"), None)
    return jax.shard_map(
        functools.partial(shards, sizes),
        mesh=mesh,
        in_specs=(rows, rows, rows, rows, rows, P(("inner", "outer"))),
        out_specs=(rows, rows, rows, rows, P(("inner", "outer"))),
        check_vma=False,
    )
```

time: 117 us -> 99.9 us (0.85)
  Pallas kernels: 107 us -> 90 us
  local copies, waits for them, and re-layouts: 3.44 us -> 4.69 us
    pallas_call x1, Pallas kernels: 107 us -> 90 us  [exchange_step(): pl.pallas_call(functools.partial(kernel, sizes), out_shape=(jax.ShapeDtyp...]
    unnamed x7 -> x11, local copies, waits for them, and re-layouts: 2.77 us -> 4.1 us
where the time goes in v3:
time: 99.9 us; the launch traced here: 99.7 us
  Pallas kernels  90 us (90%)
  local copies, waits for them, and re-layouts  4.69 us (5%)
  other arithmetic  4.25 us (4%)
    pallas_call x1, Pallas kernels, exchange_step(): pl.pallas_call(functools.partial(kernel, sizes), out_shape=(jax.ShapeDtyp...  90 us
    sub x1, other arithmetic, adam_update(): return (label_rows - 0.001 * update, new_first, new_second)  4.25 us
    unnamed x11, local copies, waits for them, and re-layouts  4.1 us

profile of v3, /device:TPU:8, one launch (start us, length us, event | category | flops | bytes accessed | tf_op | source)
XLA Modules:
  0.0 99.7 jit_solution(13160437491239296839)
XLA Ops:
  0.7 0.0 copy-start
  0.7 1.4 %copy-done = f32[512,768]{1,0:T(8,128)S(1)} copy-done((f32[512,768]{1,0:T(8,128)S(1)}, f32[512,768]{1,0:T(8,128)}, u32[]{:S(2)}) %copy-start) | copy-done | bytes 1572888
  2.1 0.0 copy-start.1
  2.1 0.7 copy-done.1
  2.8 0.0 copy-start.2
  2.8 0.7 copy-done.2
  3.5 0.0 copy-start.3
  3.5 0.7 copy-done.3
  4.1 0.0 copy-start.4
  4.2 90.0 %classifier_step.1 = (f32[512,768]{1,0:T(8,128)S(1)}, f32[16,768]{1,0:T(8,128)S(1)}, f32[8,128]{1,0:T(8,128)S(1)}) custom-call(bf16[16,768]{1,0:T(8,128)(2,1)S(1)} %copy-done.1, f32[512,768]{1,0:T(8,128)S(1)} %copy-done, s32[8,16]{1,0:T(8,128)S(1)} %bitcast.4, s32[1,16]{1,0:T(1,128)S(1)} %bitcast.5), custom_call_target="tpu_custom_call" | custom-call | tf_op jit(solution)/shard_map/classifier_step/pallas_call | solution.py:552
  94.2 0.6 dynamic-slice_bitcast_fusion
  94.8 0.0 copy-done.4
  94.8 4.3 %multiply_subtract_fusion = (f32[512,768]{1,0:T(8,128)}, f32[512,768]{1,0:T(8,128)}, f32[512,768]{1,0:T(8,128)}) fusion(f32[512,768]{1,0:T(8,128)S(1)} %copy-done, f32[512,768]{1,0:T(8,128)S(1)} %get-tuple-element.8, f32[512,768]{1,0:T(8,128)S(1)} %copy-done.4, f32[512,768]{1,0:T(8,128)} %param.9), kind=kLoop, calls=%fused_computation.2 | loop fusion | flops 5111808 | bytes 11010048 | tf_op jit(solution)/shard_map/sub | solution.py:597
  99.0 0.6 copy.12
  (1 shorter events, 0.0 us)
Async XLA Ops:
  0.7 1.4 %copy-start = (f32[512,768]{1,0:T(8,128)S(1)}, f32[512,768]{1,0:T(8,128)}, u32[]{:S(2)}) copy-start(f32[512,768]{1,0:T(8,128)} %rows_ref.1) | copy-start | bytes 4718596
  2.1 0.7 copy-start.1
  2.8 0.7 copy-start.2
  3.5 0.7 copy-start.3
  4.1 90.6 %copy-start.4 = (f32[512,768]{1,0:T(8,128)S(1)}, f32[512,768]{1,0:T(8,128)}, u32[]{:S(2)}) copy-start(f32[512,768]{1,0:T(8,128)} %param.8) | copy-start | bytes 4718596

commit v4 on v3

--- a/solution.py
+++ b/solution.py
@@ -15,6 +15,8 @@
 GATHER_ORDERS = ("zyx", "zxy", "yxz")
 LINK_RATE = 46.0
 COPIES = 320
+ADAM_TILES = 4
+ADAM_AHEAD = 4
 
 
 class Place:
@@ -85,7 +87,7 @@
                 sent.append(copy)
                 begin = max(now, free.get(message.link, 0.0))
                 free[message.link] = begin + message.kib * (message.hops if message.hops < 3 else 1.5) / LINK_RATE
-                arrivals.append((free[message.link] + 1.4 + 0.6 * message.hops, len(sent), message))
+                arrivals.append((free[message.link] + 1.8 + 0.6 * message.hops, len(sent), message))
 
     def run(job):
         nonlocal now
@@ -242,12 +244,14 @@
                 if step == 1:
                     landed = landed.at[0]
                 deps = [("out", part, 1, offset, way, step - 1)] if step > 1 else []
-                ahead, here = (
-                    [offset_of(sizes["x"], sign * (reach - step + k)) for k in (1, 0)] if first == "x" else [offset] * 2
-                )
-                deps += [("query", ahead)]
+                if first == "x":
+                    ahead, here = ([offset_of(sizes["x"], sign * (reach - step + k))] for k in (1, 0))
+                else:
+                    ahead = here = [offset] if second == "x" else offsets(sizes["x"])
+                deps += [("query", plane) for plane in ahead]
                 add(("out", part, 1, offset, way, step), first, sign, base / (1 + (step == 1)), 1, deps,
-                    functools.partial(block, 1), landed, functools.partial(block, 0), [("query", here)])
+                    functools.partial(block, 1), landed, functools.partial(block, 0),
+                    [("query", plane) for plane in here])
     for step in range(1, far + 1):
         for way, sign in enumerate((1, -1)):
 
@@ -313,8 +317,10 @@
     valid = lax.broadcasted_iota(jnp.int32, (8, 16), 0) < count_in[...]
     own_ids = jnp.where(valid, ids_in[...], -1)
     ids_own[...] = jnp.where(lane // 16 == at["z"], jnp.concatenate([own_ids] * nz, axis=1), -1)
-    loading[0].wait()
-    rows_bf[core] = rows[...].astype(jnp.bfloat16)
+
+    def cast_rows():
+        loading[0].wait()
+        rows_bf[core] = rows[...].astype(jnp.bfloat16)
 
     pl.semaphore_wait(barrier, len(peers))
 
@@ -375,8 +381,9 @@
     def rows_landed():
         return copies.copy(rows_slot, rows_bf.at[1 - core], rows_bf.at[1 - core], "core", 1)
 
-    messages.append(Message("rows", ("core", True), width * 1.5 / 4, 1, (), rows_copy, rows_landed))
+    messages.append(Message("rows", ("core", True), width * 1.5 / 4, 1, ["cast"], rows_copy, rows_landed))
     jobs = [
+        Job("cast", 0.6, (), cast_rows, 2),
         Job("merge", 0, [("ids1", delta) for delta in range(1, nz)], merge_ids),
         Job("spread", 0, ["merge", *(("ids2", delta) for delta in range(1, ny))], spread_ids),
         *(
@@ -513,7 +520,7 @@
     ))
     every_hit = [("hits", x, y) for x in range(nx) for y in range(ny)]
     jobs += [
-        Job(("query", offset), 3.0, [("combine", 2, None), *every_hit], functools.partial(query_plane, offset), 1)
+        Job(("query", offset), 1.6, [("combine", 2, None), *every_hit], functools.partial(query_plane, offset), 1)
         for offset in order
     ]
     for name, side, out in (("theirs", 1 - core, row_part), ("ours", core, row_grad_ref)):
@@ -584,27 +591,82 @@
             dma((COPIES,)), dma((COPIES,)), dma((4,)),
         ],
         compiler_params=pltpu.CompilerParams(
-            collective_id=0, has_side_effects=True, vmem_limit_bytes=46 << 20
+            collective_id=0, has_side_effects=True, vmem_limit_bytes=60 << 20
         ),
         name="classifier_step",
     )(queries, label_rows, slot_ids, counts)
 
 
-def adam_update(label_rows, first_moment, second_moment, row_grad):
-    new_first = 0.9 * first_moment + 0.1 * row_grad
-    new_second = 0.999 * second_moment + 0.001 * row_grad * row_grad
-    update = new_first / (1.0 - 0.9**10) / (jnp.sqrt(new_second / (1.0 - 0.999**10)) + 1e-08)
-    return (label_rows - 0.001 * update, new_first, new_second)
+def adam_kernel(nz, grad_ref, rows_ref, first_ref, second_ref, query_ref, log_ref,
+                new_rows_ref, new_first_ref, new_second_ref, query_grad_ref, own_ref,
+                grad, rows, first, second, new_rows, new_first, new_second, load, store):
+    count = grad.shape[0] // ADAM_TILES
+    loads = []
+    for number in range(ADAM_TILES):
+        tile = pl.ds(number * count, count)
+        pairs = ((grad_ref, grad), (rows_ref, rows), (first_ref, first), (second_ref, second))
+        loads.append([
+            pltpu.make_async_copy(source.at[tile], target.at[tile], load.at[number, k])
+            for k, (source, target) in enumerate(pairs)
+        ])
+    for copy in itertools.chain(*loads[:ADAM_AHEAD]):
+        copy.start()
+    query_grad_ref[...] = query_ref[...]
+    z = lax.rem(lax.axis_index("inner") // 2, nz)
+    own = jnp.zeros((1, 16), jnp.float32)
+    for k in range(nz):
+        own = jnp.where(z == k, log_ref[0:1, k * 16 : (k + 1) * 16], own)
+    own_ref[...] = own
+    stores = []
+    for number in range(ADAM_TILES):
+        tile = pl.ds(number * count, count)
+        for copy in itertools.chain(*loads[number + ADAM_AHEAD : number + ADAM_AHEAD + 1]):
+            copy.start()
+        for copy in loads[number]:
+            copy.wait()
+        gradient = grad[tile]
+        moment = 0.9 * first[tile] + 0.1 * gradient
+        spread = 0.999 * second[tile] + 0.001 * gradient * gradient
+        update = moment / (1.0 - 0.9**10) / (jnp.sqrt(spread / (1.0 - 0.999**10)) + 1e-08)
+        new_rows[tile] = rows[tile] - 0.001 * update
+        new_first[tile] = moment
+        new_second[tile] = spread
+        pairs = ((new_rows, new_rows_ref), (new_first, new_first_ref), (new_second, new_second_ref))
+        for k, (source, target) in enumerate(pairs):
+            copy = pltpu.make_async_copy(source.at[tile], target.at[tile], store.at[number, k])
+            copy.start()
+            stores.append(copy)
+    for copy in stores:
+        copy.wait()
+
+
+def adam_step(row_grad, label_rows, first_moment, second_moment, query_grad, logs, nz):
+    f32 = jnp.float32
+    whole = jax.ShapeDtypeStruct(label_rows.shape, f32)
+    vmem = pl.BlockSpec(memory_space=pltpu.VMEM)
+    hbm = pl.BlockSpec(memory_space=pltpu.HBM)
+    return pl.pallas_call(
+        functools.partial(adam_kernel, nz),
+        out_shape=(whole, whole, whole, jax.ShapeDtypeStruct(query_grad.shape, f32), jax.ShapeDtypeStruct((1, 16), f32)),
+        in_specs=[hbm] * 4 + [vmem] * 2,
+        out_specs=(hbm, hbm, hbm, vmem, vmem),
+        scratch_shapes=[
+            *[pltpu.VMEM(label_rows.shape, f32)] * 7,
+            pltpu.SemaphoreType.DMA((ADAM_TILES, 4)), pltpu.SemaphoreType.DMA((ADAM_TILES, 3)),
+        ],
+        compiler_params=pltpu.CompilerParams(vmem_limit_bytes=60 << 20),
+        name="adam_step",
+    )(row_grad, label_rows, first_moment, second_moment, query_grad, logs)
 
 
 def shards(sizes, queries, label_rows, first_moment, second_moment, positive_ids, positive_counts):
     row_grad, query_grad, logs = exchange_step(
         queries, label_rows, positive_ids.T, positive_counts.reshape(1, -1), sizes
     )
-    z = lax.rem(lax.axis_index("inner") // 2, sizes["z"])
-    own_total = lax.dynamic_slice_in_dim(logs[0], z * 16, 16, 0)
-    new_rows, new_first, new_second = adam_update(label_rows, first_moment, second_moment, row_grad)
-    return (new_rows, new_first, new_second, query_grad, own_total)
+    new_rows, new_first, new_second, query_grad, own_total = adam_step(
+        row_grad, label_rows, first_moment, second_moment, query_grad, logs, sizes["z"]
+    )
+    return (new_rows, new_first, new_second, query_grad, own_total.reshape(-1))
 
 
 def solution(mesh):

time: 99.9 us -> 95.7 us (0.958)
  local copies, waits for them, and re-layouts: 4.69 us -> 0 us
  Pallas kernels: 90 us -> 94.4 us
  other arithmetic: 4.25 us -> 0 us
    pallas_call x0 -> x1, Pallas kernels: none -> 6.27 us  [adam_step(): pl.pallas_call(functools.partial(adam_kernel, nz), out_shape=(whole, whol...]
    sub x1 -> x0, other arithmetic: 4.25 us -> none  [adam_update(): return (label_rows - 0.001 * update, new_first, new_second)]
    unnamed x11 -> x0, local copies, waits for them, and re-layouts: 4.1 us -> none
    pallas_call x1, Pallas kernels: 90 us -> 88.1 us  [exchange_step(): pl.pallas_call(functools.partial(kernel, sizes), out_shape=(jax.ShapeDtyp...]
where the time goes in v4:
time: 95.7 us; the launch traced here: 95.2 us
  Pallas kernels  94.4 us (99%)
    pallas_call x1, Pallas kernels, exchange_step(): pl.pallas_call(functools.partial(kernel, sizes), out_shape=(jax.ShapeDtyp...  88.1 us
    pallas_call x1, Pallas kernels, adam_step(): pl.pallas_call(functools.partial(adam_kernel, nz), out_shape=(whole, whol...  6.27 us

profile of v4, /device:TPU:8, one launch (start us, length us, event | category | flops | bytes accessed | tf_op | source)
XLA Modules:
  0.0 95.2 jit_solution(8564118185719770412)
XLA Ops:
  0.6 88.1 %classifier_step.1 = (f32[512,768]{1,0:T(8,128)}, f32[16,768]{1,0:T(8,128)}, f32[8,128]{1,0:T(8,128)}) custom-call(bf16[16,768]{1,0:T(8,128)(2,1)} %q_ref.1, f32[512,768]{1,0:T(8,128)} %rows_ref.3, s32[8,16]{1,0:T(8,128)} %bitcast.3, s32[1,16]{1,0:T(1,128)} %bitcast.4), custom_call_target="tpu_custom_call" | custom-call | tf_op jit(solution)/shard_map/classifier_step/pallas_call | solution.py:559
  88.7 6.3 %adam_step.1 = (f32[512,768]{1,0:T(8,128)}, f32[512,768]{1,0:T(8,128)}, f32[512,768]{1,0:T(8,128)}, f32[16,768]{1,0:T(8,128)}, f32[1,16]{1,0:T(1,128)}) custom-call(f32[512,768]{1,0:T(8,128)} %get-tuple-element.13.grad_ref, f32[512,768]{1,0:T(8,128)} %rows_ref.3, f32[512,768]{1,0:T(8,128)} %first_ref.1, f32[512,768]{1,0:T(8,128)} %second_ref.1, ...), custom_call_target="tpu_custom_call" | custom-call | tf_op jit(solution)/shard_map/adam_step/pallas_call | solution.py:648

commit v5 on v4

--- a/solution.py
+++ b/solution.py
@@ -59,7 +59,8 @@
 
 
 def offset_of(n, offset):
-    return n // 2 if offset == -(n // 2) else offset
+    offset = (offset + n) % n
+    return offset if offset <= n // 2 else offset - n
 
 
 class Message:
@@ -87,7 +88,7 @@
                 sent.append(copy)
                 begin = max(now, free.get(message.link, 0.0))
                 free[message.link] = begin + message.kib * (message.hops if message.hops < 3 else 1.5) / LINK_RATE
-                arrivals.append((free[message.link] + 1.8 + 0.6 * message.hops, len(sent), message))
+                arrivals.append((free[message.link] + 2.7 + 0.6 * message.hops, len(sent), message))
 
     def run(job):
         nonlocal now
@@ -175,16 +176,12 @@
         add(("in", part, 1, delta), first, delta, base, far, (), block)
     start = [("in", part, 1, delta) for delta in range(1, sizes[first])]
     base *= sizes[first]
-    reach = sizes[second] // 2
-    for step in range(1, reach + 1):
-        for way, sign in enumerate((1, -1)):
-
-            def block(back, step=step, way=way, sign=sign):
-                fixed = {third: at[third], second: place.ring(second, -sign * (step - 1 + back))}
-                return slab(held, way if step == reach else None, fixed)
-
-            deps = start if step == 1 else [("in", part, 2, way, step - 1)]
-            add(("in", part, 2, way, step), second, sign, base / (1 + (step == reach)), 1, deps, block)
+    for delta in range(1, sizes[second]):
+
+        def block(back, delta=delta):
+            return slab(held, None, {third: at[third], second: place.ring(second, -delta * back)})
+
+        add(("in", part, 2, delta), second, delta, base, min(delta, sizes[second] - delta), start, block)
     far = sizes[third] // 2
     for offset in offsets(sizes[second]):
         for step in range(1, far + 1):
@@ -201,10 +198,8 @@
                     deps = [("in", part, 3, offset, way, step - 1)]
                 elif offset == 0:
                     deps = start
-                elif abs(offset) == reach:
-                    deps = [("in", part, 2, 0, reach), ("in", part, 2, 1, reach)]
                 else:
-                    deps = [("in", part, 2, 0 if offset < 0 else 1, abs(offset))]
+                    deps = [("in", part, 2, -offset % sizes[second])]
                 add(("in", part, 3, offset, way, step), third, sign, base / (1 + (step == far)), 1, deps, block)
     return out
 

time: 95.7 us -> 94 us (0.982)
  Pallas kernels: 94.4 us -> 92.8 us
    pallas_call x1, Pallas kernels: 88.1 us -> 86.5 us  [exchange_step(): pl.pallas_call(functools.partial(kernel, sizes), out_shape=(jax.ShapeDtyp...]
where the time goes in v5:
time: 94 us; the launch traced here: 93.6 us
  Pallas kernels  92.8 us (99%)
    pallas_call x1, Pallas kernels, exchange_step(): pl.pallas_call(functools.partial(kernel, sizes), out_shape=(jax.ShapeDtyp...  86.5 us
    pallas_call x1, Pallas kernels, adam_step(): pl.pallas_call(functools.partial(adam_kernel, nz), out_shape=(whole, whol...  6.27 us

profile of v5, /device:TPU:8, one launch (start us, length us, event | category | flops | bytes accessed | tf_op | source)
XLA Modules:
  0.0 93.6 jit_solution(789779892559977121)
XLA Ops:
  0.6 86.5 %classifier_step.1 = (f32[512,768]{1,0:T(8,128)}, f32[16,768]{1,0:T(8,128)}, f32[8,128]{1,0:T(8,128)}) custom-call(bf16[16,768]{1,0:T(8,128)(2,1)} %q_ref.1, f32[512,768]{1,0:T(8,128)} %rows_ref.3, s32[8,16]{1,0:T(8,128)} %bitcast.3, s32[1,16]{1,0:T(1,128)} %bitcast.4), custom_call_target="tpu_custom_call" | custom-call | tf_op jit(solution)/shard_map/classifier_step/pallas_call | solution.py:554
  87.1 6.3 %adam_step.1 = (f32[512,768]{1,0:T(8,128)}, f32[512,768]{1,0:T(8,128)}, f32[512,768]{1,0:T(8,128)}, f32[16,768]{1,0:T(8,128)}, f32[1,16]{1,0:T(1,128)}) custom-call(f32[512,768]{1,0:T(8,128)} %get-tuple-element.13.grad_ref, f32[512,768]{1,0:T(8,128)} %rows_ref.3, f32[512,768]{1,0:T(8,128)} %first_ref.1, f32[512,768]{1,0:T(8,128)} %second_ref.1, ...), custom_call_target="tpu_custom_call" | custom-call | tf_op jit(solution)/shard_map/adam_step/pallas_call | solution.py:643

commit v6 on v5

--- a/solution.py
+++ b/solution.py
@@ -75,8 +75,8 @@
         self.key, self.cost, self.deps, self.work, self.rank = key, cost, set(deps), work, rank
 
 
-def play(messages, jobs):
-    now, free, arrivals, done, sent = 0.0, {}, [], set(), []
+def play(messages, jobs, sent):
+    now, free, arrivals, done, number = 0.0, {}, [], set(), itertools.count()
     waiting, jobs = list(messages), list(jobs)
 
     def start_ready():
@@ -85,10 +85,10 @@
                 waiting.remove(message)
                 copy = message.copy()
                 copy.start()
-                sent.append(copy)
+                sent.append((message.key if isinstance(message.key, str) else message.key[0], copy))
                 begin = max(now, free.get(message.link, 0.0))
                 free[message.link] = begin + message.kib * (message.hops if message.hops < 3 else 1.5) / LINK_RATE
-                arrivals.append((free[message.link] + 2.7 + 0.6 * message.hops, len(sent), message))
+                arrivals.append((free[message.link] + 2.7 + 0.6 * message.hops, next(number), message))
 
     def run(job):
         nonlocal now
@@ -116,7 +116,6 @@
             done.add(message.key)
         start_ready()
     assert not waiting
-    return sent
 
 
 class Copies:
@@ -526,13 +525,22 @@
             ))
             before = [(name, offset)]
     jobs.append(Job("sum", 0.5, ["row", ("ours", order[-1])], row_sum, 2))
-    sent = play(messages, jobs)
+    sent = []
+
+    def drain():
+        early = [entry for entry in sent if entry[0] not in ("out", "row")]
+        sent[:] = [entry for entry in sent if entry[0] in ("out", "row")]
+        for _, copy in early:
+            copy.wait_send()
+
+    jobs.append(Job("drain", 1.0, [("theirs", order[-1])], drain, 2))
+    play(messages, jobs, sent)
     log_ref[...] = jnp.broadcast_to(logs[at["x"], pl.ds(at["y"], 1)], (8, lanes))
     for piece in range(6):
         query_grad_ref[:, piece * LANES : (piece + 1) * LANES] = total[
             piece // 2, piece % 2, at["x"], at["y"], at["z"]
         ]
-    for copy in sent:
+    for _, copy in sent:
         copy.wait_send()
 
 

time: 94 us -> 93.8 us (level)
  no operation moved by 1% of the time
where the time goes in v6:
time: 93.8 us; the launch traced here: 93.3 us
  Pallas kernels  92.5 us (99%)
    pallas_call x1, Pallas kernels, exchange_step(): pl.pallas_call(functools.partial(kernel, sizes), out_shape=(jax.ShapeDtyp...  86.3 us
    pallas_call x1, Pallas kernels, adam_step(): pl.pallas_call(functools.partial(adam_kernel, nz), out_shape=(whole, whol...  6.27 us

profile of v6, /device:TPU:8, one launch (start us, length us, event | category | flops | bytes accessed | tf_op | source)
XLA Modules:
  0.0 93.3 jit_solution(18177466221278099101)
XLA Ops:
  0.6 86.3 %classifier_step.1 = (f32[512,768]{1,0:T(8,128)}, f32[16,768]{1,0:T(8,128)}, f32[8,128]{1,0:T(8,128)}) custom-call(bf16[16,768]{1,0:T(8,128)(2,1)} %q_ref.1, f32[512,768]{1,0:T(8,128)} %rows_ref.3, s32[8,16]{1,0:T(8,128)} %bitcast.3, s32[1,16]{1,0:T(1,128)} %bitcast.4), custom_call_target="tpu_custom_call" | custom-call | tf_op jit(solution)/shard_map/classifier_step/pallas_call | solution.py:562
  86.9 6.3 %adam_step.1 = (f32[512,768]{1,0:T(8,128)}, f32[512,768]{1,0:T(8,128)}, f32[512,768]{1,0:T(8,128)}, f32[16,768]{1,0:T(8,128)}, f32[1,16]{1,0:T(1,128)}) custom-call(f32[512,768]{1,0:T(8,128)} %get-tuple-element.13.grad_ref, f32[512,768]{1,0:T(8,128)} %rows_ref.3, f32[512,768]{1,0:T(8,128)} %first_ref.1, f32[512,768]{1,0:T(8,128)} %second_ref.1, ...), custom_call_target="tpu_custom_call" | custom-call | tf_op jit(solution)/shard_map/adam_step/pallas_call | solution.py:651
